TPU v7x, 256 devices: a whole 4x4x8 slice. The times are simulated.
256 devices in a mesh: wide: 64 (over z, y, x_hi), narrow: 4 (over x_lo, core).
Axes of the slice: x: 4 (x_hi: 2, x_lo: 2; x = x_hi * 2 + x_lo), y: 4, z: 8, core: 2. Of those that a mesh axis runs over, the one named last changes fastest.
Arguments:
- embeddings: bfloat16 [65536, 4096], P('wide', 'narrow'), may hold values from -6 to 6
- cluster_ids: int32 [65536, 1], P('wide'), may hold values from 0 to 63; in each aligned block of 1024 rows (0 to 1023, 1024 to 2047, ...) at most 32 rows name the same one
Outputs:
- gram_tiles: bfloat16 [64, 2048, 2048], P('wide', None, 'narrow')
Inputs may be any that keep to these rules, and one draw needn't show every extreme that they name: `cluster_ids`: in each aligned block of 1024 rows (the rows of one index of wide), no cluster is named by more than 32 rows, a bound that some block reaches.
All inputs are finite; a program needn't handle non-finite values.
Results may differ from a plain program's by a relative error of at most 0.0075.
Values may be sent and summed in bfloat16 or wider, within the bound.
A program may use at most 64 MiB of HBM per device.

v0:
```python
import jax
import jax.numpy as jnp
from jax import lax
from jax.sharding import PartitionSpec as P

K = 256
ITERS = 2


def orthonormal(image_rows, square):
    lower_factor = jnp.linalg.cholesky(square)
    return lax.linalg.triangular_solve(
        lower_factor, image_rows, left_side=False, lower=True, transpose_a=True
    )


def project(embeddings, basis_now):
    summand = jnp.dot(
        embeddings, basis_now.astype(jnp.bfloat16), preferred_element_type=jnp.float32
    )
    return lax.psum(summand, "narrow")


def normalize_rows(coords):
    sum_squares = jnp.sum(coords * coords, axis=1, keepdims=True)
    scale_factor = lax.rsqrt(sum_squares + 1e-06)
    return (coords * scale_factor).astype(jnp.bfloat16)


def on_device(embeddings, cluster_ids):
    narrow_count = lax.axis_size("narrow")
    wide_count = lax.axis_size("wide")
    row_count = embeddings.shape[0]
    col_count = embeddings.shape[1]
    basis_width = K
    row_pos = lax.axis_index("narrow") * col_count + jnp.arange(col_count, dtype=jnp.int32)
    col_pos = jnp.arange(basis_width, dtype=jnp.int32)
    basis_now = (row_pos[:, None] % basis_width == col_pos[None, :]).astype(jnp.float32)
    for sweep in range(ITERS):
        coords_low = project(embeddings, basis_now).astype(jnp.bfloat16)
        summand = lax.dot_general(
            embeddings, coords_low, (((0,), (0,)), ((), ())), preferred_element_type=jnp.float32
        )
        image_rows = lax.psum(summand, "wide")
        square = lax.psum(
            jnp.dot(image_rows.T, image_rows, precision=lax.Precision.HIGHEST), "narrow"
        )
        basis_now = orthonormal(image_rows, square)
    coords = project(embeddings, basis_now)
    unit_rows = normalize_rows(coords)
    owner_ids = cluster_ids[:, 0]
    onehot = (owner_ids[:, None] == jnp.arange(wide_count, dtype=jnp.int32)[None, :]).astype(
        jnp.int32
    )
    slot_index = jnp.sum((jnp.cumsum(onehot, axis=0) - onehot) * onehot, axis=1)
    capacity = max(4, 2 * row_count // wide_count)
    target = slot_index * wide_count + owner_ids
    outgoing = (
        jnp.zeros((capacity * wide_count, basis_width), jnp.bfloat16).at[target].set(unit_rows)
    )
    outgoing = outgoing.reshape(capacity, wide_count, basis_width)
    arrived = lax.all_to_all(outgoing, "wide", split_axis=1, concat_axis=1, tiled=True)
    members = arrived.reshape(capacity * wide_count, basis_width)
    column_count = members.shape[0] // narrow_count
    own_rows = lax.dynamic_slice_in_dim(
        members, lax.axis_index("narrow") * column_count, column_count, 0
    )
    gram_tile = lax.dot_general(
        members, own_rows, (((1,), (1,)), ((), ())), preferred_element_type=jnp.float32
    )
    return gram_tile.astype(jnp.bfloat16)[None]


def solution(mesh):
    in_specs = (P("wide", "narrow"), P("wide", None))
    out_specs = P("wide", None, "narrow")
    return jax.shard_map(
        on_device, mesh=mesh, in_specs=in_specs, out_specs=out_specs, check_vma=False
    )
```

profile of v0, /device:TPU:1, one launch (start us, length us, event | category | flops | bytes accessed | tf_op | source)
XLA Modules:
  0.0 1798.5 jit_solution(10847504549548937843)
XLA Ops:
  6.6 1.6 copy-done
  8.1 2.0 convolution_bitcast_fusion.4
  10.1 29.2 %all-reduce.18 = bf16[1024,256]{0,1:T(8,128)(2,1)S(1)} all-reduce(f32[1024,256]{0,1:T(8,128)} %convolution_bitcast_fusion.4), channel_id=1, replica_groups=mesh['wide'=64,'narrow'=4] {'narrow'}, use_global_device_ids=true, to_apply=%region_3.4 | all-reduce | flops 262144 | bytes 1572864 | tf_op jit(solution)/shard_map/psum | solution.py:21
  39.3 1.7 convolution_bitcast_fusion.3
  41.0 653.6 %all-reduce.9.cloned.1.call-done = f32[1024,256]{0,1:T(8,128)} async-done(((f32[1024,256]{0,1:T(8,128)}), f32[1024,256]{0,1:T(8,128)}) %all-reduce.9.cloned.1.call-update) | async-done | bytes 1048592 | tf_op jit(solution)/shard_map/psum | solution.py:44
  694.7 3.3 fusion.40
  698.6 82.7 %all-reduce.11.cloned.1.call-done = f32[256,256]{0,1:T(8,128)} async-done(((f32[256,256]{0,1:T(8,128)}), f32[256,256]{0,1:T(8,128)}) %all-reduce.11.cloned.1.call-update) | async-done | bytes 262160 | tf_op jit(solution)/shard_map/psum | solution.py:45
  781.3 1.1 copy.28
  782.3 1.0 fusion.14
  783.3 0.7 copy-done.6
  784.0 11.7 cholesky.130
  795.8 9.8 custom-call.13
  805.6 1.0 constant_dynamic-update-slice_fusion.3
  806.7 1.1 convolution_subtract_fusion.3
  807.8 11.7 cholesky.147
  819.6 0.7 compare_reduce_fusion.2
  821.5 1.0 select_select_fusion.1
  822.6 4.3 while.4
  822.8 0.6 fusion.64
  823.4 1.4 bitcast_dynamic-update-slice_fusion.4
  824.9 0.6 fusion.64
  825.4 1.4 bitcast_dynamic-update-slice_fusion.4
  826.9 20.3 %custom-call.14 = f32[2,128,128]{1,2,0:T(8,128)} custom-call(f32[2,128,128]{2,1,0:T(8,128)S(1)} %get-tuple-element.21), custom_call_target="InvertDiagBlocksLowerTriangular" | custom-call | tf_op jit(solution)/shard_map/triangular_solve/custom-call.0 | solution.py:12
  847.2 1.5 fusion.3
  848.7 0.6 convolution_subtract_fusion.1
  849.4 0.6 fusion.21
  850.0 0.8 convolution_bitcast_fusion.2
  850.8 26.0 %all-reduce.19 = bf16[1024,256]{0,1:T(8,128)(2,1)} all-reduce(f32[1024,256]{0,1:T(8,128)S(1)} %convolution_bitcast_fusion.2), channel_id=1, replica_groups=mesh['wide'=64,'narrow'=4] {'narrow'}, use_global_device_ids=true, to_apply=%region_10.13 | all-reduce | flops 262144 | bytes 1572864 | tf_op jit(solution)/shard_map/psum | solution.py:21
  876.8 2.7 convolution_bitcast_fusion.1
  879.6 653.2 %all-reduce.13.cloned.1.call-done = f32[1024,256]{0,1:T(8,128)} async-done(((f32[1024,256]{0,1:T(8,128)}), f32[1024,256]{0,1:T(8,128)}) %all-reduce.13.cloned.1.call-update) | async-done | bytes 1048592 | tf_op jit(solution)/shard_map/psum | solution.py:44
  1532.7 3.3 fusion.41
  1536.3 83.0 %all-reduce.15.cloned.1.call-done = f32[256,256]{0,1:T(8,128)} async-done(((f32[256,256]{0,1:T(8,128)}), f32[256,256]{0,1:T(8,128)}) %all-reduce.15.cloned.1.call-update) | async-done | bytes 262160 | tf_op jit(solution)/shard_map/psum | solution.py:45
  1619.3 1.1 copy.31
  1620.4 1.0 fusion.13
  1621.4 0.7 copy-done.5
  1622.1 11.7 cholesky.164
  1633.9 0.7 compare_reduce_fusion.1
  1634.6 9.8 custom-call.15
  1644.4 1.0 constant_dynamic-update-slice_fusion.1
  1645.5 1.1 convolution_subtract_fusion.2
  1646.6 11.7 cholesky.181
  1658.3 0.6 compare_reduce_fusion
  1660.2 1.0 select_select_fusion
  1661.2 4.4 while.5
  1661.5 0.6 fusion.65
  1662.1 1.4 bitcast_dynamic-update-slice_fusion.5
  1663.6 0.6 fusion.65
  1664.2 1.4 bitcast_dynamic-update-slice_fusion.5
  1665.6 20.3 %custom-call.16 = f32[2,128,128]{1,2,0:T(8,128)} custom-call(f32[2,128,128]{2,1,0:T(8,128)S(1)} %get-tuple-element.22), custom_call_target="InvertDiagBlocksLowerTriangular" | custom-call | tf_op jit(solution)/shard_map/triangular_solve/custom-call.0 | solution.py:12
  1685.9 1.5 fusion.1
  1687.5 0.6 convolution_subtract_fusion
  1688.1 0.6 fusion.17
  1688.7 1.7 convolution_bitcast_fusion
  1690.5 18.0 %reduce-window.6 = s32[64,8,128]{2,1,0:T(8,128)S(1)} reduce-window(s32[64,8,128]{2,1,0:T(8,128)S(1)} %fusion.16, s32[]{:T(128)} %constant.85.clone.1), window={size=1x1x128 pad=0_0x0_0x127_0}, to_apply=%region_0.1 | reduce-window | flops 8323072 | bytes 524292 | tf_op jit(solution)/shard_map/reduce-window
  1709.2 28.9 %all-reduce.17.cloned.1.call-done = f32[1024,256]{0,1:T(8,128)} async-done(((f32[1024,256]{0,1:T(8,128)}), f32[1024,256]{0,1:T(8,128)}) %all-reduce.17.cloned.1.call-update) | async-done | bytes 1048592 | tf_op jit(solution)/shard_map/psum | solution.py:21
  1738.0 1.3 multiply_reduce_fusion
  1739.4 1.3 multiply_convert_fusion
  1740.7 1.0 copy.33
  1741.7 5.7 scatter_custom_fusion
  1747.4 1.6 copy.34
  1748.9 12.3 all-to-all-start
  1761.3 27.8 %all-to-all-done = bf16[32,64,256]{2,0,1:T(8,128)(2,1)S(1)} async-done(((bf16[32,64,256]{2,0,1:T(8,128)(2,1)}), bf16[32,64,256]{2,0,1:T(8,128)(2,1)S(1)}, u32[]{:S(2)}, u32[]{:S(2)}) %all-to-all-start) | async-done | bytes 1048608 | tf_op jit(solution)/shard_map/all_to_all | solution.py:62
  1789.0 0.6 copy.35
  1789.6 2.1 fusion
  (55 shorter events, 2.0 us)
Async XLA Ops:
  6.5 1.6 copy-start
  6.5 688.1 %all-reduce.9.cloned.1.call-start = ((), (), s32[]{:S(2)}) async-start(), calls=%async_computation.1 | async-start | bytes 2097152 | tf_op jit(solution)/shard_map/psum | solution.py:44
  41.0 740.3 %all-reduce.11.cloned.1.call-start = ((), (), s32[]{:S(2)}) async-start(), calls=%async_computation.2 | async-start | bytes 524288 | tf_op jit(solution)/shard_map/psum | solution.py:45
  698.0 149.2 %copy-start.1 = (f32[1024,256]{0,1:T(8,128)S(1)}, f32[1024,256]{0,1:T(8,128)}, u32[]{:S(2)}) copy-start(f32[1024,256]{0,1:T(8,128)} %all-reduce.9.cloned.1.call-done) | copy-start | bytes 3145732
  698.0 834.8 %all-reduce.13.cloned.1.call-start = ((), (), s32[]{:S(2)}) async-start(), calls=%async_computation.3 | async-start | bytes 2097152 | tf_op jit(solution)/shard_map/psum | solution.py:44
  783.3 0.7 copy-start.6
  819.5 2.0 copy-start.3
  847.2 2.2 copy-start.7
  879.5 739.8 %all-reduce.15.cloned.1.call-start = ((), (), s32[]{:S(2)}) async-start(), calls=%async_computation.4 | async-start | bytes 524288 | tf_op jit(solution)/shard_map/psum | solution.py:45
  1536.0 149.9 %copy-start.2 = (f32[1024,256]{0,1:T(8,128)S(1)}, f32[1024,256]{0,1:T(8,128)}, u32[]{:S(2)}) copy-start(f32[1024,256]{0,1:T(8,128)} %all-reduce.13.cloned.1.call-done) | copy-start | bytes 3145732
  1536.1 202.0 %all-reduce.17.cloned.1.call-start = ((), (), s32[]{:S(2)}) async-start(), calls=%async_computation.5 | async-start | bytes 2097152 | tf_op jit(solution)/shard_map/psum | solution.py:21
  1621.4 0.7 copy-start.5
  1658.3 1.9 copy-start.4
  1685.9 2.2 copy-start.8
  1688.7 1.8 copy-start.9
  1748.9 40.1 %all-to-all-start = ((bf16[32,64,256]{2,0,1:T(8,128)(2,1)}), bf16[32,64,256]{2,0,1:T(8,128)(2,1)S(1)}, u32[]{:S(2)}, u32[]{:S(2)}) async-start(bf16[32,64,256]{2,0,1:T(8,128)(2,1)} %copy.34), calls=%async_computation | async-start | bytes 2097152 | tf_op jit(solution)/shard_map/all_to_all | solution.py:62
Sparse Core Ops, SparseCore 0:
  41.1 653.5 all-reduce.8
  698.1 83.1 all-reduce.10
  879.7 653.0 all-reduce.12
  1536.2 83.1 all-reduce.14
  1690.6 47.3 all-reduce.16
where the time goes:
time: 1800 us
  waiting for transfers between devices  1530 us (85%)
  other arithmetic  134 us (7%)
  blocking collectives  55.2 us (3%)
  matrix products  27.3 us (2%)
  local copies, waits for them, and re-layouts  22.6 us (1%)
    psum x2, waiting for transfers between devices, on_device(): image_rows = lax.psum(summand, 'wide')  1310 us
    psum x2, waiting for transfers between devices, on_device(): lax.psum(jnp.dot(image_rows.T, image_rows, precision=lax.Precision.HIGHES...  166 us
    another operation x13, other arithmetic, orthonormal(): lower_factor = jnp.linalg.cholesky(square)  68.7 us
    psum x2, blocking collectives, project(): return lax.psum(summand, 'narrow')  55.2 us
    another operation x5, other arithmetic, orthonormal(): lax.linalg.triangular_solve(lower_factor, image_rows, left_side=False, lo...  42.6 us
  transfers between devices with their start and end apart: 6, of which 6 were waited for; matrix products, arithmetic and copies ran while one was open for 1% of the time, Pallas kernels for 0%

commit v1 on v0

v1 whole, which is shorter than its diff:
```python
import jax
import jax.numpy as jnp
from jax import lax
from jax.experimental import pallas as pl
from jax.experimental.pallas import tpu as pltpu
from jax.sharding import PartitionSpec as P

F32 = jnp.float32
BF16 = jnp.bfloat16
HIGHEST = lax.Precision.HIGHEST
MESH = pl.DeviceIdType.MESH

K = 256
ITERS = 2
HALF = 128
PANEL = 16
CHUNKS = 4
WIDE = 64
PIECE = 16
SLOTS = 32


def dot(a, b, dims, precision=None):
    return lax.dot_general(
        a, b, (dims, ((), ())), precision=precision, preferred_element_type=F32
    )


NN = ((1,), (0,))
NT = ((1,), (1,))


def split3(x):
    a = x.astype(BF16)
    rest = x - a.astype(F32)
    b = rest.astype(BF16)
    c = (rest - b.astype(F32)).astype(BF16)
    return a, b, c


def eliminate(m):
    n = HALF
    sub = lax.broadcasted_iota(jnp.int32, (PANEL, n), 0)
    for r0 in range(0, n, PANEL):
        left = m[r0 : r0 + PANEL, 0:n]
        right = m[r0 : r0 + PANEL, n : 2 * n]
        cols = [
            jnp.broadcast_to(left[:, r0 + j : r0 + j + 1], (PANEL, n)) for j in range(PANEL)
        ]
        scale = jnp.zeros((PANEL, n), F32)
        for j in range(PANEL):
            pivot = cols[j][j : j + 1, :]
            factor = jnp.where(sub > j, cols[j] * (1.0 / pivot), 0.0)
            for k in range(j + 1, PANEL):
                cols[k] = cols[k] - factor * cols[k][j : j + 1, :]
            left = left - factor * left[j : j + 1, :]
            right = right - factor * right[j : j + 1, :]
            scale = jnp.where(sub == j, lax.rsqrt(jnp.broadcast_to(pivot, (PANEL, n))), scale)
        left = left * scale
        right = right * scale
        m[r0 : r0 + PANEL, 0:n] = left
        m[r0 : r0 + PANEL, n : 2 * n] = right
        r1 = r0 + PANEL
        if r1 < n:
            a, b, c = (t.astype(F32) for t in split3(jnp.concatenate([left, right], axis=1)))
            rows = jnp.concatenate([a, a, b, b, a, c], axis=0)[:, 0:n].T[r1:].astype(BF16)
            pivots = jnp.concatenate([a, b, a, b, c, a], axis=0).astype(BF16)
            m[r1:n, :] = m[r1:n, :] - dot(rows, pivots, NN)


def inverse_factor(square, m, out):
    n = HALF
    row = lax.broadcasted_iota(jnp.int32, (n, n), 0)
    col = lax.broadcasted_iota(jnp.int32, (n, n), 1)
    eye = jnp.where(row == col, 1.0, 0.0).astype(F32)
    m[:, 0:n] = square[0:n, 0:n]
    m[:, n : 2 * n] = eye
    eliminate(m)
    first = m[:, n : 2 * n]
    lower = dot(square[n:, 0:n], first, NT, HIGHEST)
    out[0:n, 0:n] = first
    out[0:n, n:] = jnp.zeros((n, n), F32)
    cross = dot(lower, first, NN, HIGHEST)
    m[:, 0:n] = square[n:, n:] - dot(lower, lower, NT, HIGHEST)
    m[:, n : 2 * n] = eye
    eliminate(m)
    second = m[:, n : 2 * n]
    out[n:, n:] = second
    out[n:, 0:n] = -dot(second, cross, NN, HIGHEST)


def kernel(
    a_ref,
    ids_ref,
    out_ref,
    vt,
    place,
    part,
    send1,
    recv1,
    chip,
    send2,
    recv2,
    low,
    full,
    acc,
    ys,
    yr,
    yg,
    sq,
    sqr1,
    sqt,
    sqr2,
    sqf,
    work,
    linv,
    outgoing,
    arrived,
    wide_f32,
    by_lane,
    s1,
    q1,
    s2,
    q2,
    s3,
    q3,
    s4,
    q4,
    ws,
    wq,
    gs,
    gq,
    es,
    eq,
    ts,
    tq,
    fs,
    fq,
):
    w = lax.axis_index("wide")
    n = lax.axis_index("narrow")
    core = lax.rem(n, 2)
    other = 1 - core
    core_peer = n + 1 - 2 * core
    chip_peer = lax.rem(n + 2, 4)

    def to(src, dst, send, recv, wide, narrow):
        return pltpu.make_async_remote_copy(
            src_ref=src,
            dst_ref=dst,
            send_sem=send,
            recv_sem=recv,
            device_id={"wide": wide, "narrow": narrow},
            device_id_type=MESH,
        )

    barrier = pltpu.get_barrier_semaphore()

    @pl.loop(1, WIDE)
    def _(i):
        pl.semaphore_signal(
            barrier, inc=1, device_id={"wide": lax.rem(w + i, WIDE), "narrow": n}, device_id_type=MESH
        )

    pl.semaphore_signal(barrier, inc=1, device_id={"wide": w, "narrow": core_peer}, device_id_type=MESH)
    pl.semaphore_signal(barrier, inc=1, device_id={"wide": w, "narrow": chip_peer}, device_id_type=MESH)

    rows = a_ref.shape[0]
    ids = ids_ref[...]
    cluster = lax.broadcasted_iota(jnp.int32, (WIDE, rows), 0)
    onehot = jnp.where(cluster == ids, 1.0, 0.0).astype(F32)
    earlier = jnp.where(
        lax.broadcasted_iota(jnp.int32, (rows, rows), 0)
        < lax.broadcasted_iota(jnp.int32, (rows, rows), 1),
        1.0,
        0.0,
    ).astype(BF16)
    counts = dot(onehot.astype(BF16), earlier, NN)
    slot = jnp.sum(counts * onehot, axis=0, keepdims=True).astype(jnp.int32)
    mine = slot - core * PIECE
    target = jnp.where((mine >= 0) & (mine < PIECE), ids * PIECE + mine, -1)

    @pl.loop(0, WIDE * PIECE, step=128)
    def _(r):
        position = lax.broadcasted_iota(jnp.int32, (128, rows), 0) + r
        place[pl.ds(r, 128), :] = jnp.where(position == target, 1.0, 0.0).astype(BF16)

    row = lax.broadcasted_iota(jnp.int32, (K, K), 0)
    col = lax.broadcasted_iota(jnp.int32, (K, K), 1)
    eye = jnp.where(row == col, 1.0, 0.0).astype(BF16)
    for g in range(CHUNKS):
        vt[:, g * K : (g + 1) * K] = eye

    pl.semaphore_wait(barrier, WIDE - 1 + 2)

    def project(it, final):
        def c1(g):
            return to(send1.at[it, g], recv1.at[it, g], s1.at[it, g], q1.at[it, g], w, core_peer)

        def c2(g):
            return to(send2.at[it, g], recv2.at[it, g], s2.at[it, g], q2.at[it, g], w, chip_peer)

        def c3(g, half):
            if final:
                block = full.at[half, g]
                return to(block, block, s4.at[g], q4.at[g], w, core_peer)
            block = low.at[it, half, g]
            return to(block, block, s3.at[it, g], q3.at[it, g], w, core_peer)

        for g in range(CHUNKS):
            now = dot(vt[...], a_ref[g * K : (g + 1) * K, :], NT)
            part[g, 0] = now[0:HALF]
            part[g, 1] = now[HALF:]
            send1[it, g] = part[g, other].astype(BF16)
            c1(g).start()
        for g in range(CHUNKS):
            c1(g).wait_recv()
            now = part[g, core] + recv1[it, g].astype(F32)
            chip[g] = now
            send2[it, g] = now.astype(BF16)
            c2(g).start()
        for g in range(CHUNKS):
            c2(g).wait_recv()
            now = chip[g] + recv2[it, g].astype(F32)
            if final:
                full[core, g] = now
            else:
                low[it, core, g] = now.astype(BF16)
            c3(g, core).start()
        return c1, c2, c3

    def sweep(it, carry):
        c1, c2, c3 = project(it, False)
        for g in range(CHUNKS):
            c3(g, other).wait_recv()
            lower = jnp.concatenate([low[it, 0, g], low[it, 1, g]], axis=0)
            for q in range(CHUNKS):
                now = dot(lower, a_ref[g * K : (g + 1) * K, q * K : (q + 1) * K], NN)
                if g > 0:
                    now = now + acc[q]
                if g < CHUNKS - 1:
                    acc[q] = now
                else:
                    ys[it, q * PIECE : (q + 1) * PIECE] = now.astype(BF16).reshape(
                        PIECE, PIECE, K
                    )

        def scatter(i):
            there = lax.rem(w + i, WIDE)
            return to(ys.at[it, there], yr.at[it, w], ws.at[it], wq.at[it], there, n)

        def gather(i):
            there = lax.rem(w + i, WIDE)
            return to(yg.at[it, w], yg.at[it, w], gs.at[it], gq.at[it], there, n)

        def drain(buffer, sem):
            block = buffer.at[it, pl.ds(0, WIDE - 1)]
            pltpu.make_async_copy(block, block, sem.at[it]).wait()

        @pl.loop(1, WIDE)
        def _(i):
            scatter(i).start()

        yr[it, w] = ys[it, w]
        for g in range(CHUNKS):
            c1(g).wait_send()
            c2(g).wait_send()
            c3(g, core).wait_send()
        drain(yr, wq)
        total = lax.fori_loop(
            0,
            WIDE,
            lambda j, t: t + yr[it, j].astype(F32),
            jnp.zeros((PIECE, K), F32),
            unroll=8,
        )
        yg[it, w] = total.astype(BF16)

        @pl.loop(1, WIDE)
        def _(i):
            gather(i).start()

        drain(ys, ws)
        drain(yg, gq)

        images = [yg[it, q * PIECE : (q + 1) * PIECE].reshape(K, K) for q in range(CHUNKS)]
        now = dot(images[0], images[0], NT)
        for q in range(1, CHUNKS):
            now = now + dot(images[q], images[q], NT)
        sq[0] = now[0:HALF]
        sq[1] = now[HALF:]

        e1 = to(sq.at[other], sqr1.at[it], es.at[it, 0], eq.at[it, 0], w, core_peer)
        e1.start()
        e1.wait_recv()
        sqt[...] = sq[core] + sqr1[it]
        e2 = to(sqt, sqr2.at[it], es.at[it, 1], eq.at[it, 1], w, chip_peer)
        e2.start()
        e2.wait_recv()
        mine = sqf.at[it, pl.ds(core * HALF, HALF)]
        mine[...] = sqt[...] + sqr2[it]
        e3 = to(mine, mine, es.at[it, 2], eq.at[it, 2], w, core_peer)
        e3.start()
        e3.wait_recv()
        inverse_factor(sqf.at[it], work, linv)
        a, b, c = split3(linv[...])
        for q in range(CHUNKS):
            y = yg[it, q * PIECE : (q + 1) * PIECE].reshape(K, K)
            vt[:, q * K : (q + 1) * K] = (
                dot(a, y, NN) + (dot(b, y, NN) + dot(c, y, NN))
            ).astype(BF16)
        e1.wait_send()
        e2.wait_send()
        e3.wait_send()
        drain(yg, gs)
        return carry

    lax.fori_loop(0, ITERS, sweep, 0)

    c1, c2, c3 = project(ITERS, True)
    for g in range(CHUNKS):
        c3(g, other).wait_recv()
        coords = jnp.concatenate([full[0, g], full[1, g]], axis=0)
        scale = lax.rsqrt(jnp.sum(coords * coords, axis=0, keepdims=True) + 1e-06)
        unit = (coords * scale).astype(BF16)
        now = dot(place[:, g * K : (g + 1) * K], unit, NT)
        if g > 0:
            now = now + wide_f32[...]
        if g < CHUNKS - 1:
            wide_f32[...] = now
        else:
            outgoing[...] = now.astype(BF16).reshape(WIDE, PIECE, K)

    def deliver(i):
        there = lax.rem(w + i, WIDE)
        return to(outgoing.at[there], arrived.at[core, w], ts, tq, there, n)

    @pl.loop(1, WIDE)
    def _(i):
        deliver(i).start()

    arrived[core, w] = outgoing[w]
    for g in range(CHUNKS):
        c1(g).wait_send()
        c2(g).wait_send()
        c3(g, core).wait_send()
    block = arrived.at[core, pl.ds(0, WIDE - 1)]
    pltpu.make_async_copy(block, block, tq).wait()
    forward = to(arrived.at[core], arrived.at[core], fs, fq, w, core_peer)
    forward.start()

    def arrange(half):
        for h in range(2):
            lanes = slice(h * HALF, (h + 1) * HALF)
            by_lane[h] = arrived[half, :, :, lanes].astype(F32).reshape(WIDE * PIECE, HALF)
            for s in range(PIECE):
                out_ref[pl.ds((half * PIECE + s) * WIDE, WIDE), lanes] = by_lane.at[h][
                    pl.ds(s, WIDE, stride=PIECE), :
                ].astype(BF16)

    arrange(core)
    to(arrived.at[other], arrived.at[other], fs, fq, w, core_peer).wait_recv()
    arrange(other)
    forward.wait_send()
    sent = outgoing.at[pl.ds(0, WIDE - 1)]
    pltpu.make_async_copy(sent, sent, ts).wait()


def members_of(embeddings, ids):
    n_it = ITERS + 1
    dma = pltpu.SemaphoreType.DMA
    vmem = pl.BlockSpec(memory_space=pltpu.VMEM)
    return pl.pallas_call(
        kernel,
        out_shape=jax.ShapeDtypeStruct((WIDE * SLOTS, K), BF16),
        in_specs=[vmem, vmem],
        out_specs=vmem,
        scratch_shapes=[
            pltpu.VMEM((K, CHUNKS * K), BF16),
            pltpu.VMEM((WIDE * PIECE, CHUNKS * K), BF16),
            pltpu.VMEM((CHUNKS, 2, HALF, K), F32),
            pltpu.VMEM((n_it, CHUNKS, HALF, K), BF16),
            pltpu.VMEM((n_it, CHUNKS, HALF, K), BF16),
            pltpu.VMEM((CHUNKS, HALF, K), F32),
            pltpu.VMEM((n_it, CHUNKS, HALF, K), BF16),
            pltpu.VMEM((n_it, CHUNKS, HALF, K), BF16),
            pltpu.VMEM((ITERS, 2, CHUNKS, HALF, K), BF16),
            pltpu.VMEM((2, CHUNKS, HALF, K), F32),
            pltpu.VMEM((CHUNKS, K, K), F32),
            pltpu.VMEM((ITERS, WIDE, PIECE, K), BF16),
            pltpu.VMEM((ITERS, WIDE, PIECE, K), BF16),
            pltpu.VMEM((ITERS, WIDE, PIECE, K), BF16),
            pltpu.VMEM((2, HALF, K), F32),
            pltpu.VMEM((ITERS, HALF, K), F32),
            pltpu.VMEM((HALF, K), F32),
            pltpu.VMEM((ITERS, HALF, K), F32),
            pltpu.VMEM((ITERS, K, K), F32),
            pltpu.VMEM((HALF, 2 * HALF), F32),
            pltpu.VMEM((K, K), F32),
            pltpu.VMEM((WIDE, PIECE, K), BF16),
            pltpu.VMEM((2, WIDE, PIECE, K), BF16),
            pltpu.VMEM((WIDE * PIECE, K), F32),
            pltpu.VMEM((2, WIDE * PIECE, HALF), F32),
            dma((n_it, CHUNKS)),
            dma((n_it, CHUNKS)),
            dma((n_it, CHUNKS)),
            dma((n_it, CHUNKS)),
            dma((ITERS, CHUNKS)),
            dma((ITERS, CHUNKS)),
            dma((CHUNKS,)),
            dma((CHUNKS,)),
            dma((ITERS,)),
            dma((ITERS,)),
            dma((ITERS,)),
            dma((ITERS,)),
            dma((ITERS, 3)),
            dma((ITERS, 3)),
            dma,
            dma,
            dma,
            dma,
        ],
        compiler_params=pltpu.CompilerParams(
            collective_id=0, has_side_effects=True, vmem_limit_bytes=48 * 1024 * 1024
        ),
        name="sketch",
    )(embeddings, ids)


def on_device(embeddings, cluster_ids):
    members = members_of(embeddings, cluster_ids.reshape(1, -1))
    count = members.shape[0] // lax.axis_size("narrow")
    own = lax.dynamic_slice_in_dim(members, lax.axis_index("narrow") * count, count, 0)
    return dot(members, own, NT).astype(BF16)[None]


def solution(mesh):
    return jax.shard_map(
        on_device,
        mesh=mesh,
        in_specs=(P("wide", "narrow"), P("wide", None)),
        out_specs=P("wide", None, "narrow"),
        check_vma=False,
    )
```

time: 1800 us -> 166 us (0.09)
  waiting for transfers between devices: 1530 us -> 0 us
  Pallas kernels: 0 us -> 162 us
  other arithmetic: 134 us -> 0 us
  blocking collectives: 55.2 us -> 0 us
  matrix products: 27.3 us -> 2.07 us
  local copies, waits for them, and re-layouts: 22.6 us -> 2.28 us
    psum x5 -> x0, waiting for transfers between devices: 1500 us -> none  [the longest x2 1310 us: on_device(): image_rows = lax.psum(summand, 'wide')]
    pallas_call x0 -> x1, Pallas kernels: none -> 162 us  [members_of(): pl.pallas_call(kernel, out_shape=jax.ShapeDtypeStruct((WIDE * SLOTS, K),...]
    another operation x21 -> x0, other arithmetic: 129 us -> none  [the longest x13 68.7 us: orthonormal(): lower_factor = jnp.linalg.cholesky(square)]
    psum x2 -> x0, blocking collectives: 55.2 us -> none  [project(): return lax.psum(summand, 'narrow')]
    all_to_all x1 -> x0, waiting for transfers between devices: 27.8 us -> none  [on_device(): lax.all_to_all(outgoing, 'wide', split_axis=1, concat_axis=1, tiled=True)]
  transfers between devices with their start and end apart: 6 -> 0, of which waited for: 6 -> 0; matrix products, arithmetic and copies ran while one was open for 1% -> 0% of each run, Pallas kernels for 0% -> 0%
where the time goes in v1:
time: 166 us
  Pallas kernels  162 us (98%)
  local copies, waits for them, and re-layouts  2.28 us (1%)
  matrix products  2.07 us (1%)
    pallas_call x1, Pallas kernels, members_of(): pl.pallas_call(kernel, out_shape=jax.ShapeDtypeStruct((WIDE * SLOTS, K),...  162 us

profile of v1, /device:TPU:1, one launch (start us, length us, event | category | flops | bytes accessed | tf_op | source)
XLA Modules:
  0.0 165.9 jit_solution(12485110354979757426)
XLA Ops:
  0.0 0.0 copy-start
  0.0 1.6 copy-done
  1.6 0.0 copy-start.1
  1.6 0.7 copy-done.1
  2.3 161.5 %sketch.1 = bf16[2048,256]{1,0:T(8,128)(2,1)S(1)} custom-call(bf16[1024,1024]{1,0:T(8,128)(2,1)S(1)} %copy-done, s32[1,1024]{1,0:T(1,128)S(1)} %bitcast.4), custom_call_target="tpu_custom_call" | custom-call | tf_op jit(solution)/shard_map/sketch/pallas_call | solution.py:373
  163.8 2.1 %fusion = bf16[1,2048,512]{2,1,0:T(8,128)(2,1)} fusion(bf16[2048,256]{1,0:T(8,128)(2,1)S(1)} %sketch.1, s32[]{:T(128)S(6)} %select_n.3), kind=kOutput, calls=%fused_computation.1 | convolution fusion | flops 537919488 | bytes 3407876 | tf_op jit(solution)/shard_map/dot_general | solution.py:24
Async XLA Ops:
  0.0 1.6 copy-start
  1.6 0.7 copy-start.1

commit v2 on v1

v2 whole, which is shorter than its diff:
```python
import jax
import jax.numpy as jnp
from jax import lax
from jax.experimental import pallas as pl
from jax.experimental.pallas import tpu as pltpu
from jax.sharding import PartitionSpec as P

F32 = jnp.float32
BF16 = jnp.bfloat16
HIGHEST = lax.Precision.HIGHEST
MESH = pl.DeviceIdType.MESH

K = 256
ITERS = 2
HALF = 128
PANEL = 16
CHUNKS = 4
WIDE = 64
PIECE = 16
SLOTS = 32
RING = 4
PLANE = 16


def dot(a, b, dims, precision=None):
    return lax.dot_general(
        a, b, (dims, ((), ())), precision=precision, preferred_element_type=F32
    )


NN = ((1,), (0,))
NT = ((1,), (1,))


def split2(x):
    a = x.astype(BF16)
    return a, (x - a.astype(F32)).astype(BF16)


def split3(x):
    a = x.astype(BF16)
    b, c = split2(x - a.astype(F32))
    return a, b, c


def eliminate(m):
    n = HALF
    sub = lax.broadcasted_iota(jnp.int32, (PANEL, n), 0)
    for r0 in range(0, n, PANEL):
        left = m[r0 : r0 + PANEL, 0:n]
        right = m[r0 : r0 + PANEL, n : 2 * n]
        cols = [
            jnp.broadcast_to(left[:, r0 + j : r0 + j + 1], (PANEL, n)) for j in range(PANEL)
        ]
        scale = jnp.zeros((PANEL, n), F32)
        for j in range(PANEL):
            pivot = cols[j][j : j + 1, :]
            factor = jnp.where(sub > j, cols[j] * (1.0 / pivot), 0.0)
            for k in range(j + 1, PANEL):
                cols[k] = cols[k] - factor * cols[k][j : j + 1, :]
            left = left - factor * left[j : j + 1, :]
            right = right - factor * right[j : j + 1, :]
            scale = jnp.where(sub == j, lax.rsqrt(jnp.broadcast_to(pivot, (PANEL, n))), scale)
        left = left * scale
        right = right * scale
        m[r0 : r0 + PANEL, 0:n] = left
        m[r0 : r0 + PANEL, n : 2 * n] = right
        r1 = r0 + PANEL
        if r1 < n:
            a, b, c = (t.astype(F32) for t in split3(jnp.concatenate([left, right], axis=1)))
            rows = jnp.concatenate([a, a, b, b, a, c], axis=0)[:, 0:n].T[r1:].astype(BF16)
            pivots = jnp.concatenate([a, b, a, b, c, a], axis=0).astype(BF16)
            m[r1:n, :] = m[r1:n, :] - dot(rows, pivots, NN)


def inverse_factor_start(square, m, out, cross):
    n = HALF
    row = lax.broadcasted_iota(jnp.int32, (n, n), 0)
    col = lax.broadcasted_iota(jnp.int32, (n, n), 1)
    eye = jnp.where(row == col, 1.0, 0.0).astype(F32)
    m[:, 0:n] = square[0:n, 0:n]
    m[:, n : 2 * n] = eye
    eliminate(m)
    first = m[:, n : 2 * n]
    lower = dot(square[n:, 0:n], first, NT, HIGHEST)
    out[0:n, 0:n] = first
    out[0:n, n:] = jnp.zeros((n, n), F32)
    cross[...] = dot(lower, first, NN, HIGHEST)
    m[:, 0:n] = square[n:, n:] - dot(lower, lower, NT, HIGHEST)
    m[:, n : 2 * n] = eye


def inverse_factor_end(m, out, cross):
    n = HALF
    eliminate(m)
    second = m[:, n : 2 * n]
    out[n:, n:] = second
    out[n:, 0:n] = -dot(second, cross[...], NN, HIGHEST)


def kernel(
    a_hbm,
    ids_ref,
    out_ref,
    a_ref,
    vt,
    place,
    part,
    recv1,
    chip,
    send2,
    recv2,
    full,
    coords,
    low,
    ys,
    yr1,
    own,
    ysb,
    yr2,
    mine4,
    yg,
    sq,
    sqr1,
    sqt,
    sqr2,
    sqf,
    work,
    cross,
    linv,
    outgoing,
    arrived,
    by_lane,
    load_sem,
    s1,
    q1,
    s2,
    q2,
    s3,
    q3,
    as_,
    aq,
    bs,
    bq,
    cs,
    cq,
    ds,
    dq,
    es,
    eq,
    ts,
    tq,
    fs,
    fq,
):
    w = lax.axis_index("wide")
    n = lax.axis_index("narrow")
    core = lax.rem(n, 2)
    other = 1 - core
    core_peer = n + 1 - 2 * core
    chip_peer = lax.rem(n + 2, 4)
    z = w // 8
    y = lax.rem(w // 2, RING)
    x = lax.rem(w, 2)
    plane = z * 2 + x
    quad = z // 2
    within = lax.rem(plane, RING)

    def at(there, ring):
        return (there // 2) * 8 + ring * 2 + lax.rem(there, 2)

    def to(src, dst, send, recv, wide, narrow):
        return pltpu.make_async_remote_copy(
            src_ref=src,
            dst_ref=dst,
            send_sem=send,
            recv_sem=recv,
            device_id={"wide": wide, "narrow": narrow},
            device_id_type=MESH,
        )

    def settle(block, sem):
        pltpu.make_async_copy(block, block, sem).wait()

    def load(g):
        piece = pl.ds(g * K, K)
        return pltpu.make_async_copy(a_hbm.at[piece], a_ref.at[piece], load_sem.at[g])

    for g in range(CHUNKS):
        load(g).start()

    barrier = pltpu.get_barrier_semaphore()

    @pl.loop(1, WIDE)
    def _(i):
        pl.semaphore_signal(
            barrier,
            inc=1,
            device_id={"wide": lax.rem(w + i, WIDE), "narrow": n},
            device_id_type=MESH,
        )

    for peer in (core_peer, chip_peer):
        pl.semaphore_signal(
            barrier, inc=1, device_id={"wide": w, "narrow": peer}, device_id_type=MESH
        )

    row = lax.broadcasted_iota(jnp.int32, (K, K), 0)
    col = lax.broadcasted_iota(jnp.int32, (K, K), 1)
    eye = jnp.where(row == col, 1.0, 0.0).astype(BF16)
    for g in range(CHUNKS):
        vt[:, g * K : (g + 1) * K] = eye

    def c1(it, g):
        return to(part.at[g, other], recv1.at[it, g], s1.at[it, g], q1.at[it, g], w, core_peer)

    def c2(it, g):
        return to(send2.at[it, g], recv2.at[it, g], s2.at[it, g], q2.at[it, g], w, chip_peer)

    def c3(it, g, half):
        block = full.at[it, g, half]
        return to(block, block, s3.at[it, g], q3.at[it, g], w, core_peer)

    def project(g):
        now = dot(vt[...], a_ref[g * K : (g + 1) * K, :], NT)
        part[g, 0] = now[0:HALF]
        part[g, 1] = now[HALF:]

    def over_cores(it, g):
        c1(it, g).wait_recv()
        now = part[g, core] + recv1[it, g]
        chip[g] = now
        send2[it, g] = now.astype(BF16)
        c2(it, g).start()

    def over_chips(it, g):
        c2(it, g).wait_recv()
        full[it, g, core] = chip[g] + recv2[it, g].astype(F32)
        c3(it, g, core).start()

    def whole(it, g):
        c3(it, g, other).wait_recv()
        return jnp.concatenate([full[it, g, 0], full[it, g, 1]], axis=0)

    def sent(it):
        for g in range(CHUNKS):
            c1(it, g).wait_send()
            c2(it, g).wait_send()
            c3(it, g, core).wait_send()

    for g in range(CHUNKS):
        load(g).wait()
        project(g)
        if g == 0:
            pl.semaphore_wait(barrier, WIDE - 1 + 2)
        c1(0, g).start()
    for g in range(CHUNKS):
        over_cores(0, g)

    rows = a_ref.shape[0]
    ids = ids_ref[...]
    cluster = lax.broadcasted_iota(jnp.int32, (WIDE, rows), 0)
    onehot = jnp.where(cluster == ids, 1.0, 0.0).astype(F32)
    earlier = jnp.where(
        lax.broadcasted_iota(jnp.int32, (rows, rows), 0)
        < lax.broadcasted_iota(jnp.int32, (rows, rows), 1),
        1.0,
        0.0,
    ).astype(BF16)
    counts = dot(onehot.astype(BF16), earlier, NN)
    slot = jnp.sum(counts * onehot, axis=0, keepdims=True).astype(jnp.int32)
    offset = slot - core * PIECE
    target = jnp.where((offset >= 0) & (offset < PIECE), ids * PIECE + offset, -1)

    @pl.loop(0, WIDE * PIECE, step=128)
    def _(r):
        position = lax.broadcasted_iota(jnp.int32, (128, rows), 0) + r
        place[pl.ds(r, 128), :] = jnp.where(position == target, 1.0, 0.0).astype(BF16)

    for g in range(CHUNKS):
        over_chips(0, g)
    for g in range(CHUNKS):
        low[:, g * K : (g + 1) * K] = whole(0, g).astype(BF16)
    sent(0)

    def sweep(it, carry):
        def first(off, c, k):
            piece = pl.ds(c * RING, RING)
            return to(
                ys.at[it, off - 1, piece],
                yr1.at[it, off - 1, piece],
                as_.at[it],
                aq.at[it, k],
                at(plane, lax.rem(y + off, RING)),
                n,
            )

        order = (2, 1, 3, 0)
        for off in order:
            q = lax.rem(y + off, RING)
            now = dot(low[...], a_ref[:, pl.ds(pl.multiple_of(q * K, K), K)], NN)
            if off:
                ys[it, off - 1] = now.astype(BF16).reshape(PLANE, PIECE, K)
                for k, turn in enumerate(order):
                    first(off, lax.rem(quad + turn, RING), k).start()
            else:
                own[...] = now.reshape(PLANE, PIECE, K)

        for k, turn in enumerate(order):
            c = lax.rem(quad + turn, RING)
            settle(yr1.at[it, :, pl.ds(0, RING)], aq.at[it, k])
            piece = pl.ds(c * RING, RING)
            now = own[piece]
            for off in (1, 2, 3):
                now = now + yr1[it, off - 1, piece].astype(F32)
            ysb[it, piece] = now.astype(BF16)
            if turn == 0:
                mine4[...] = now
            for t in range(0 if turn else 1, RING):
                there = c * RING + lax.rem(within + t, RING)
                to(ysb.at[it, there], yr2.at[it, plane], bs.at[it], bq.at[it], at(there, y), n).start()
        settle(yr2.at[it, pl.ds(0, PLANE - 1)], bq.at[it])
        total = mine4[within]
        for t in range(1, PLANE):
            total = total + yr2[it, lax.rem(plane + t, PLANE)].astype(F32)
        mine = yg.at[it, y * PLANE + plane]
        mine[...] = total.astype(BF16)

        @pl.loop(1, PLANE)
        def _(t):
            there = lax.rem(plane + t, PLANE)
            block = yg.at[it, y * PLANE + plane]
            to(block, block, cs.at[it], cq.at[it, quad], at(there, y), n).start()

        for turn in (0, 1, 3, 2):
            c = lax.rem(quad + turn, RING)
            settle(yg.at[it, pl.ds(0, RING if turn else RING - 1)], cq.at[it, c])
            block = yg.at[it, pl.ds(y * PLANE + c * RING, RING)]
            for off in (2, 1, 3):
                ring = lax.rem(y + off, RING)
                to(block, block, ds.at[it], dq.at[it, off - 1], at(plane, ring), n).start()
        for off in (0, 1, 3, 2):
            q = lax.rem(y - off + RING, RING)
            if off:
                settle(yg.at[it, pl.ds(0, PLANE)], dq.at[it, off - 1])
            vt[:, pl.ds(pl.multiple_of(q * K, K), K)] = yg[it, pl.ds(q * PLANE, PLANE)].reshape(K, K)

        now = dot(vt[...], vt[...], NT)
        sq[0] = now[0:HALF]
        sq[1] = now[HALF:]
        e1 = to(sq.at[other], sqr1.at[it], es.at[it, 0], eq.at[it, 0], w, core_peer)
        e1.start()
        later = it + 1
        for g in range(CHUNKS):
            project(g)
            c1(later, g).start()
        e1.wait_recv()
        sqt[...] = sq[core] + sqr1[it]
        e2 = to(sqt, sqr2.at[it], es.at[it, 1], eq.at[it, 1], w, chip_peer)
        e2.start()
        for g in range(CHUNKS):
            over_cores(later, g)
        e2.wait_recv()
        half = sqf.at[it, pl.ds(core * HALF, HALF)]
        half[...] = sqt[...] + sqr2[it]
        e3 = to(half, half, es.at[it, 2], eq.at[it, 2], w, core_peer)
        e3.start()
        rest = sqf.at[it, pl.ds(other * HALF, HALF)]
        to(rest, rest, es.at[it, 2], eq.at[it, 2], w, core_peer).wait_recv()
        inverse_factor_start(sqf.at[it], work, linv, cross)
        for g in range(CHUNKS):
            over_chips(later, g)
        inverse_factor_end(work, linv, cross)
        a, b = split2(linv[...])
        for g in range(CHUNKS):
            c, d = split2(whole(later, g))
            now = dot(a, c, NN) + (dot(a, d, NN) + dot(b, c, NN))
            coords[g] = now
            low[:, g * K : (g + 1) * K] = now.astype(BF16)

        sent(later)
        e1.wait_send()
        e2.wait_send()
        e3.wait_send()
        settle(ys.at[it], as_.at[it])
        settle(ysb.at[it, pl.ds(0, PLANE - 1)], bs.at[it])
        settle(yg.at[it, pl.ds(0, PLANE - 1)], cs.at[it])
        settle(ys.at[it], ds.at[it])
        return carry

    lax.fori_loop(0, ITERS, sweep, 0)

    for g in range(CHUNKS):
        now = coords[g]
        scale = lax.rsqrt(jnp.sum(now * now, axis=0, keepdims=True) + 1e-06)
        low[:, g * K : (g + 1) * K] = (now * scale).astype(BF16)
    outgoing[...] = dot(place[...], low[...], NT).astype(BF16).reshape(WIDE, PIECE, K)

    @pl.loop(1, WIDE)
    def _(i):
        there = lax.rem(w + i, WIDE)
        to(outgoing.at[there], arrived.at[core, w], ts, tq, there, n).start()

    arrived[core, w] = outgoing[w]
    settle(arrived.at[core, pl.ds(0, WIDE - 1)], tq)
    forward = to(arrived.at[core], arrived.at[core], fs, fq, w, core_peer)
    forward.start()

    def arrange(half):
        for h in range(2):
            lanes = slice(h * HALF, (h + 1) * HALF)
            by_lane[h] = arrived[half, :, :, lanes].astype(F32).reshape(WIDE * PIECE, HALF)
            for s in range(PIECE):
                out_ref[pl.ds((half * PIECE + s) * WIDE, WIDE), lanes] = by_lane.at[h][
                    pl.ds(s, WIDE, stride=PIECE), :
                ].astype(BF16)

    arrange(core)
    to(arrived.at[other], arrived.at[other], fs, fq, w, core_peer).wait_recv()
    arrange(other)
    forward.wait_send()
    settle(outgoing.at[pl.ds(0, WIDE - 1)], ts)


def members_of(embeddings, ids):
    n_it = ITERS + 1
    dma = pltpu.SemaphoreType.DMA
    vmem = pl.BlockSpec(memory_space=pltpu.VMEM)
    return pl.pallas_call(
        kernel,
        out_shape=jax.ShapeDtypeStruct((WIDE * SLOTS, K), BF16),
        in_specs=[pl.BlockSpec(memory_space=pl.ANY), vmem],
        out_specs=vmem,
        scratch_shapes=[
            pltpu.VMEM((CHUNKS * K, CHUNKS * K), BF16),
            pltpu.VMEM((K, CHUNKS * K), BF16),
            pltpu.VMEM((WIDE * PIECE, CHUNKS * K), BF16),
            pltpu.VMEM((CHUNKS, 2, HALF, K), F32),
            pltpu.VMEM((n_it, CHUNKS, HALF, K), F32),
            pltpu.VMEM((CHUNKS, HALF, K), F32),
            pltpu.VMEM((n_it, CHUNKS, HALF, K), BF16),
            pltpu.VMEM((n_it, CHUNKS, HALF, K), BF16),
            pltpu.VMEM((n_it, CHUNKS, 2, HALF, K), F32),
            pltpu.VMEM((CHUNKS, K, K), F32),
            pltpu.VMEM((K, CHUNKS * K), BF16),
            pltpu.VMEM((ITERS, RING - 1, PLANE, PIECE, K), BF16),
            pltpu.VMEM((ITERS, RING - 1, PLANE, PIECE, K), BF16),
            pltpu.VMEM((PLANE, PIECE, K), F32),
            pltpu.VMEM((ITERS, PLANE, PIECE, K), BF16),
            pltpu.VMEM((ITERS, PLANE, PIECE, K), BF16),
            pltpu.VMEM((RING, PIECE, K), F32),
            pltpu.VMEM((ITERS, WIDE, PIECE, K), BF16),
            pltpu.VMEM((2, HALF, K), F32),
            pltpu.VMEM((ITERS, HALF, K), F32),
            pltpu.VMEM((HALF, K), F32),
            pltpu.VMEM((ITERS, HALF, K), F32),
            pltpu.VMEM((ITERS, K, K), F32),
            pltpu.VMEM((HALF, 2 * HALF), F32),
            pltpu.VMEM((HALF, HALF), F32),
            pltpu.VMEM((K, K), F32),
            pltpu.VMEM((WIDE, PIECE, K), BF16),
            pltpu.VMEM((2, WIDE, PIECE, K), BF16),
            pltpu.VMEM((2, WIDE * PIECE, HALF), F32),
            dma((CHUNKS,)),
            *[dma((n_it, CHUNKS))] * 6,
            dma((ITERS,)),
            dma((ITERS, RING)),
            dma((ITERS,)),
            dma((ITERS,)),
            dma((ITERS,)),
            dma((ITERS, RING)),
            dma((ITERS,)),
            dma((ITERS, RING - 1)),
            dma((ITERS, 3)),
            dma((ITERS, 3)),
            dma,
            dma,
            dma,
            dma,
        ],
        compiler_params=pltpu.CompilerParams(
            collective_id=0, has_side_effects=True, vmem_limit_bytes=56 * 1024 * 1024
        ),
        name="sketch",
    )(embeddings, ids)


def on_device(embeddings, cluster_ids):
    members = members_of(embeddings, cluster_ids.reshape(1, -1))
    count = members.shape[0] // lax.axis_size("narrow")
    own = lax.dynamic_slice_in_dim(members, lax.axis_index("narrow") * count, count, 0)
    return dot(members, own, NT).astype(BF16)[None]


def solution(mesh):
    return jax.shard_map(
        on_device,
        mesh=mesh,
        in_specs=(P("wide", "narrow"), P("wide", None)),
        out_specs=P("wide", None, "narrow"),
        check_vma=False,
    )
```

time: 166 us -> 137 us (0.83)
  Pallas kernels: 162 us -> 133 us
  local copies, waits for them, and re-layouts: 2.28 us -> 0 us
    pallas_call x1, Pallas kernels: 162 us -> 133 us  [members_of(): pl.pallas_call(kernel, out_shape=jax.ShapeDtypeStruct((WIDE * SLOTS, K),...]
    unnamed x4 -> x0, local copies, waits for them, and re-layouts: 2.28 us -> none
where the time goes in v2:
time: 137 us
  Pallas kernels  133 us (97%)
  matrix products  3.33 us (2%)
    pallas_call x1, Pallas kernels, members_of(): pl.pallas_call(kernel, out_shape=jax.ShapeDtypeStruct((WIDE * SLOTS, K),...  133 us
    dot_general x1, matrix products, dot(): lax.dot_general(a, b, (dims, ((), ())), precision=precision, preferred_el...  3.33 us

profile of v2, /device:TPU:1, one launch (start us, length us, event | category | flops | bytes accessed | tf_op | source)
XLA Modules:
  0.0 136.7 jit_solution(11052723376571352265)
XLA Ops:
  0.0 133.4 %sketch.1 = bf16[2048,256]{1,0:T(8,128)(2,1)} custom-call(bf16[1024,1024]{1,0:T(8,128)(2,1)} %a_hbm.1, s32[1,1024]{1,0:T(1,128)} %bitcast.4), custom_call_target="tpu_custom_call" | custom-call | tf_op jit(solution)/shard_map/sketch/pallas_call | solution.py:429
  133.4 3.3 %fusion = bf16[1,2048,512]{2,1,0:T(8,128)(2,1)} fusion(bf16[2048,256]{1,0:T(8,128)(2,1)} %sketch.1, s32[]{:T(128)S(6)} %select_n.3), kind=kOutput, calls=%fused_computation.1 | convolution fusion | flops 537919488 | bytes 3407876 | tf_op jit(solution)/shard_map/dot_general | solution.py:26

commit v3 on v2

v3 whole, which is shorter than its diff:
```python
import jax
import jax.numpy as jnp
from jax import lax
from jax.experimental import pallas as pl
from jax.experimental.pallas import tpu as pltpu
from jax.sharding import PartitionSpec as P

F32 = jnp.float32
BF16 = jnp.bfloat16
HIGHEST = lax.Precision.HIGHEST
MESH = pl.DeviceIdType.MESH

K = 256
ITERS = 2
HALF = 128
PANEL = 16
CHUNKS = 4
WIDE = 64
PIECE = 16
SLOTS = 32
RING = 4
PLANE = 16
QUARTER = 8


def dot(a, b, dims, precision=None):
    return lax.dot_general(
        a, b, (dims, ((), ())), precision=precision, preferred_element_type=F32
    )


NN = ((1,), (0,))
NT = ((1,), (1,))


def split2(x):
    a = x.astype(BF16)
    return a, (x - a.astype(F32)).astype(BF16)


def split3(x):
    a = x.astype(BF16)
    b, c = split2(x - a.astype(F32))
    return a, b, c


def eliminate(m, between=None):
    n = HALF
    sub = lax.broadcasted_iota(jnp.int32, (PANEL, n), 0)
    for r0 in range(0, n, PANEL):
        left = m[r0 : r0 + PANEL, 0:n]
        right = m[r0 : r0 + PANEL, n : 2 * n]
        cols = [
            jnp.broadcast_to(left[:, r0 + j : r0 + j + 1], (PANEL, n)) for j in range(PANEL)
        ]
        scale = jnp.zeros((PANEL, n), F32)
        for j in range(PANEL):
            pivot = cols[j][j : j + 1, :]
            factor = jnp.where(sub > j, cols[j] * (1.0 / pivot), 0.0)
            for k in range(j + 1, PANEL):
                cols[k] = cols[k] - factor * cols[k][j : j + 1, :]
            left = left - factor * left[j : j + 1, :]
            right = right - factor * right[j : j + 1, :]
            scale = jnp.where(sub == j, lax.rsqrt(jnp.broadcast_to(pivot, (PANEL, n))), scale)
        left = left * scale
        right = right * scale
        m[r0 : r0 + PANEL, 0:n] = left
        m[r0 : r0 + PANEL, n : 2 * n] = right
        r1 = r0 + PANEL
        if r1 < n:
            a, b, c = (t.astype(F32) for t in split3(jnp.concatenate([left, right], axis=1)))
            rows = jnp.concatenate([a, a, b, b, a, c], axis=0)[:, 0:n].T[r1:].astype(BF16)
            pivots = jnp.concatenate([a, b, a, b, c, a], axis=0).astype(BF16)
            m[r1:n, :] = m[r1:n, :] - dot(rows, pivots, NN)
        if between is not None:
            between(r0 // PANEL)


def inverse_factor_start(square, m, out, cross):
    n = HALF
    row = lax.broadcasted_iota(jnp.int32, (n, n), 0)
    col = lax.broadcasted_iota(jnp.int32, (n, n), 1)
    eye = jnp.where(row == col, 1.0, 0.0).astype(F32)
    m[:, 0:n] = square[0:n, 0:n]
    m[:, n : 2 * n] = eye
    eliminate(m)
    first = m[:, n : 2 * n]
    lower = dot(square[n:, 0:n], first, NT, HIGHEST)
    out[0:n, 0:n] = first
    out[0:n, n:] = jnp.zeros((n, n), F32)
    cross[...] = dot(lower, first, NN, HIGHEST)
    m[:, 0:n] = square[n:, n:] - dot(lower, lower, NT, HIGHEST)
    m[:, n : 2 * n] = eye


def inverse_factor_end(m, out, cross, between):
    n = HALF
    eliminate(m, between)
    second = m[:, n : 2 * n]
    out[n:, n:] = second
    out[n:, 0:n] = -dot(second, cross[...], NN, HIGHEST)


def to(src, dst, send, recv, wide, narrow):
    return pltpu.make_async_remote_copy(
        src_ref=src,
        dst_ref=dst,
        send_sem=send,
        recv_sem=recv,
        device_id={"wide": wide, "narrow": narrow},
        device_id_type=MESH,
    )


def settle(block, sem):
    pltpu.make_async_copy(block, block, sem).wait()


def signal(barrier, wide, narrow):
    pl.semaphore_signal(
        barrier, inc=1, device_id={"wide": wide, "narrow": narrow}, device_id_type=MESH
    )


def sum_over_narrow(w, n, vt, a_ref, part, recv1, chip, send2, recv2, full, sems):
    core = lax.rem(n, 2)
    other = 1 - core
    core_peer = n + 1 - 2 * core
    chip_peer = lax.rem(n + 2, 4)
    s1, q1, s2, q2, s3, q3 = sems

    def c1(it, g):
        return to(part.at[g, other], recv1.at[it, g], s1.at[it, g], q1.at[it, g], w, core_peer)

    def c2(it, g):
        return to(send2.at[it, g], recv2.at[it, g], s2.at[it, g], q2.at[it, g], w, chip_peer)

    def c3(it, g, half):
        block = full.at[it, g, half]
        return to(block, block, s3.at[it, g], q3.at[it, g], w, core_peer)

    def project(it, g):
        now = dot(vt[...], a_ref[g * K : (g + 1) * K, :], NT)
        part[g, 0] = now[0:HALF]
        part[g, 1] = now[HALF:]
        c1(it, g).start()

    def over_cores(it, g):
        c1(it, g).wait_recv()
        now = part[g, core] + recv1[it, g]
        chip[g] = now
        send2[it, g] = now.astype(BF16)
        c2(it, g).start()

    def over_chips(it, g):
        c2(it, g).wait_recv()
        full[it, g, core] = chip[g] + recv2[it, g].astype(F32)
        c3(it, g, core).start()

    def whole(it, g):
        c3(it, g, other).wait_recv()
        return jnp.concatenate([full[it, g, 0], full[it, g, 1]], axis=0)

    def sent(it):
        for g in range(CHUNKS):
            c1(it, g).wait_send()
            c2(it, g).wait_send()
            c3(it, g, core).wait_send()

    return project, over_cores, over_chips, whole, sent


def first_kernel(
    a_hbm,
    ids_ref,
    a_ref,
    low_ref,
    place,
    vt,
    part,
    recv1,
    chip,
    send2,
    recv2,
    full,
    load_sem,
    s1,
    q1,
    s2,
    q2,
    s3,
    q3,
):
    w = lax.axis_index("wide")
    n = lax.axis_index("narrow")
    barrier = pltpu.get_barrier_semaphore()
    signal(barrier, w, n + 1 - 2 * lax.rem(n, 2))
    signal(barrier, w, lax.rem(n + 2, 4))

    def load(g):
        piece = pl.ds(g * K, K)
        return pltpu.make_async_copy(a_hbm.at[piece], a_ref.at[piece], load_sem.at[g])

    for g in range(CHUNKS):
        load(g).start()
    row = lax.broadcasted_iota(jnp.int32, (K, K), 0)
    col = lax.broadcasted_iota(jnp.int32, (K, K), 1)
    eye = jnp.where(row == col, 1.0, 0.0).astype(BF16)
    for g in range(CHUNKS):
        vt[:, g * K : (g + 1) * K] = eye
    project, over_cores, over_chips, whole, sent = sum_over_narrow(
        w, n, vt, a_ref, part, recv1, chip, send2, recv2, full, (s1, q1, s2, q2, s3, q3)
    )
    pl.semaphore_wait(barrier, 2)
    for g in range(CHUNKS):
        load(g).wait()
        project(0, g)
    for g in range(CHUNKS):
        over_cores(0, g)
    rows = a_ref.shape[0]
    ids = ids_ref[...]
    cluster = lax.broadcasted_iota(jnp.int32, (WIDE, rows), 0)
    onehot = jnp.where(cluster == ids, 1.0, 0.0).astype(F32)
    earlier = jnp.where(
        lax.broadcasted_iota(jnp.int32, (rows, rows), 0)
        < lax.broadcasted_iota(jnp.int32, (rows, rows), 1),
        1.0,
        0.0,
    ).astype(BF16)
    counts = dot(onehot.astype(BF16), earlier, NN)
    slot = jnp.sum(counts * onehot, axis=0, keepdims=True).astype(jnp.int32)
    offset = slot - n * QUARTER
    owner = ((ids >> 1) & 3) * PLANE + (ids >> 3) * 2 + (ids & 1)
    target = jnp.where((offset >= 0) & (offset < QUARTER), owner * QUARTER + offset, -1)

    @pl.loop(0, WIDE * QUARTER, step=128)
    def _(r):
        position = lax.broadcasted_iota(jnp.int32, (128, rows), 0) + r
        place[pl.ds(r, 128), :] = jnp.where(position == target, 1.0, 0.0).astype(BF16)
    for g in range(CHUNKS):
        over_chips(0, g)
    for g in range(CHUNKS):
        low_ref[:, g * K : (g + 1) * K] = whole(0, g).astype(BF16)
    sent(0)


def kernel(
    a_ref,
    low_ref,
    place,
    out_ref,
    vt,
    part,
    recv1,
    chip,
    send2,
    recv2,
    full,
    coords,
    low,
    ys,
    yr1,
    own,
    ysb,
    yr2,
    mine4,
    yg,
    sq,
    sqr1,
    sqt,
    sqr2,
    sqf,
    work,
    cross,
    linv,
    outgoing,
    arrived,
    by_lane,
    s1,
    q1,
    s2,
    q2,
    s3,
    q3,
    as_,
    aq,
    bs,
    bq,
    cs,
    cq,
    ds,
    dq,
    es,
    eq,
    ts,
    tq,
    vs,
    vq,
    fs,
    fq,
    gs,
):
    w = lax.axis_index("wide")
    n = lax.axis_index("narrow")
    core = lax.rem(n, 2)
    other = 1 - core
    core_peer = n + 1 - 2 * core
    chip_peer = lax.rem(n + 2, 4)
    z = w // 8
    y = lax.rem(w // 2, RING)
    x = lax.rem(w, 2)
    plane = z * 2 + x
    quad = z // 2
    within = lax.rem(plane, RING)

    def at(there, ring):
        return (there // 2) * 8 + ring * 2 + lax.rem(there, 2)

    barrier = pltpu.get_barrier_semaphore()

    @pl.loop(1, PLANE)
    def _(t):
        signal(barrier, at(lax.rem(plane + t, PLANE), y), n)

    for off in range(1, RING):
        signal(barrier, at(plane, lax.rem(y + off, RING)), n)
    signal(barrier, w, core_peer)
    signal(barrier, w, chip_peer)
    project, over_cores, over_chips, whole, sent = sum_over_narrow(
        w, n, vt, a_ref, part, recv1, chip, send2, recv2, full, (s1, q1, s2, q2, s3, q3)
    )
    low[...] = low_ref[...]
    pl.semaphore_wait(barrier, PLANE - 1 + RING - 1 + 2)

    def sweep(it, carry):
        def first(off, c, k):
            piece = pl.ds(c * RING, RING)
            return to(
                ys.at[it, off - 1, piece],
                yr1.at[it, off - 1, piece],
                as_.at[it],
                aq.at[it, k],
                at(plane, lax.rem(y + off, RING)),
                n,
            )

        order = (2, 1, 3, 0)
        for off in order:
            q = lax.rem(y + off, RING)
            now = dot(low[...], a_ref[:, pl.ds(pl.multiple_of(q * K, K), K)], NN)
            if off:
                ys[it, off - 1] = now.astype(BF16).reshape(PLANE, PIECE, K)
            else:
                own[...] = now.reshape(PLANE, PIECE, K)
            if off == 3:
                for k, turn in enumerate(order):
                    for there in (2, 1, 3):
                        first(there, lax.rem(quad + turn, RING), k).start()

        for k, turn in enumerate(order):
            c = lax.rem(quad + turn, RING)
            settle(yr1.at[it, :, pl.ds(0, RING)], aq.at[it, k])
            piece = pl.ds(c * RING, RING)
            now = own[piece]
            for off in (1, 2, 3):
                now = now + yr1[it, off - 1, piece].astype(F32)
            ysb[it, piece] = now.astype(BF16)
            if turn == 0:
                mine4[...] = now
            for t in range(0 if turn else 1, RING):
                there = c * RING + lax.rem(within + t, RING)
                to(ysb.at[it, there], yr2.at[it, plane], bs.at[it], bq.at[it], at(there, y), n).start()
        settle(yr2.at[it, pl.ds(0, PLANE - 1)], bq.at[it])
        total = mine4[within]
        for t in range(1, PLANE):
            total = total + yr2[it, lax.rem(plane + t, PLANE)].astype(F32)
        mine = yg.at[it, y * PLANE + plane]
        mine[...] = total.astype(BF16)

        @pl.loop(1, PLANE)
        def _(t):
            there = lax.rem(plane + t, PLANE)
            block = yg.at[it, y * PLANE + plane]
            to(block, block, cs.at[it], cq.at[it, quad], at(there, y), n).start()

        for turn in (0, 1, 3, 2):
            c = lax.rem(quad + turn, RING)
            settle(yg.at[it, pl.ds(0, RING if turn else RING - 1)], cq.at[it, c])
            block = yg.at[it, pl.ds(y * PLANE + c * RING, RING)]
            for off in (2, 1, 3):
                ring = lax.rem(y + off, RING)
                to(block, block, ds.at[it], dq.at[it, off - 1], at(plane, ring), n).start()
        for off in (0, 1, 3, 2):
            q = lax.rem(y - off + RING, RING)
            if off:
                settle(yg.at[it, pl.ds(0, PLANE)], dq.at[it, off - 1])
            vt[:, pl.ds(pl.multiple_of(q * K, K), K)] = yg[it, pl.ds(q * PLANE, PLANE)].reshape(K, K)

        now = dot(vt[...], vt[...], NT)
        sq[0] = now[0:HALF]
        sq[1] = now[HALF:]
        e1 = to(sq.at[other], sqr1.at[it], es.at[it, 0], eq.at[it, 0], w, core_peer)
        e1.start()
        for g in range(CHUNKS):
            project(it, g)
        e1.wait_recv()
        sqt[...] = sq[core] + sqr1[it]
        e2 = to(sqt, sqr2.at[it], es.at[it, 1], eq.at[it, 1], w, chip_peer)
        e2.start()
        e2.wait_recv()
        half = sqf.at[it, pl.ds(core * HALF, HALF)]
        half[...] = sqt[...] + sqr2[it]
        e3 = to(half, half, es.at[it, 2], eq.at[it, 2], w, core_peer)
        e3.start()
        for g in range(CHUNKS):
            over_cores(it, g)
        rest = sqf.at[it, pl.ds(other * HALF, HALF)]
        to(rest, rest, es.at[it, 2], eq.at[it, 2], w, core_peer).wait_recv()
        inverse_factor_start(sqf.at[it], work, linv, cross)


        def between(panel):
            if panel in (3, 4, 5, 6):
                over_chips(it, panel - 3)

        inverse_factor_end(work, linv, cross, between)
        a, b = split2(linv[...])
        for g in range(CHUNKS):
            c, d = split2(whole(it, g))
            now = dot(a, c, NN) + (dot(a, d, NN) + dot(b, c, NN))
            coords[g] = now
            low[:, g * K : (g + 1) * K] = now.astype(BF16)

        sent(it)
        e1.wait_send()
        e2.wait_send()
        e3.wait_send()
        settle(ys.at[it], as_.at[it])
        settle(ysb.at[it, pl.ds(0, PLANE - 1)], bs.at[it])
        settle(yg.at[it, pl.ds(0, PLANE - 1)], cs.at[it])
        settle(ys.at[it], ds.at[it])
        return carry

    lax.fori_loop(0, ITERS, sweep, 0)

    for g in range(CHUNKS):
        now = coords[g]
        scale = lax.rsqrt(jnp.sum(now * now, axis=0, keepdims=True) + 1e-06)
        low[:, g * K : (g + 1) * K] = (now * scale).astype(BF16)
    now = dot(place[...], low[...], NT).reshape(RING, PLANE, QUARTER, K)
    outgoing[...] = jnp.concatenate([now[..., 0:HALF], now[..., HALF:]], axis=2).astype(BF16)

    for turn in (0, 1, 3, 2):
        c = lax.rem(quad + turn, RING)

        @pl.loop(0, PLANE)
        def _(t):
            ring = lax.rem(y + t, RING)
            there = c * RING + lax.rem(within + t // RING, RING)

            def send():
                to(
                    outgoing.at[ring, there],
                    arrived.at[n, z, y, x],
                    ts,
                    tq.at[quad],
                    at(there, ring),
                    n,
                ).start()

            if turn == 0:
                pl.when(t > 0)(send)
            else:
                send()

    arrived[n, z, y, x] = outgoing[y, plane]

    def share(c, who, peer, send, recv):
        block = arrived.at[who, pl.ds(c * 2, 2)]
        return to(block, block, send, recv, w, peer)

    for turn in (0, 1, 3, 2):
        c = lax.rem(quad + turn, RING)
        count = PLANE if turn else PLANE - 1
        settle(outgoing.at[0, pl.ds(0, count)], tq.at[c])
        share(c, n, chip_peer, vs, vq.at[c]).start()
        share(c, n, core_peer, fs, fq.at[0]).start()

    def arrange(who):
        by_lane[...] = arrived[who].astype(F32).reshape(WIDE * PIECE, HALF)
        for h in range(2):
            for s in range(QUARTER):
                out_ref[
                    pl.ds((who * QUARTER + s) * WIDE, WIDE), h * HALF : (h + 1) * HALF
                ] = by_lane[pl.ds(h * QUARTER + s, WIDE, stride=PIECE), :].astype(BF16)

    arrange(n)
    for turn in (0, 1, 3, 2):
        c = lax.rem(quad + turn, RING)
        share(c, chip_peer, chip_peer, vs, vq.at[c]).wait_recv()
        share(c, chip_peer, core_peer, gs, fq.at[1]).start()
    settle(arrived.at[core_peer], fq.at[0])
    arrange(core_peer)
    arrange(chip_peer)
    last = lax.rem(core_peer + 2, 4)
    settle(arrived.at[last], fq.at[1])
    arrange(last)
    settle(arrived.at[n], fs)
    settle(arrived.at[n], vs)
    settle(arrived.at[n], gs)
    for _ in range(RING - 1):
        settle(outgoing.at[0], ts)
    settle(outgoing.at[0, pl.ds(0, PLANE - 1)], ts)


def members_of(embeddings, ids):
    dma = pltpu.SemaphoreType.DMA
    vmem = pl.BlockSpec(memory_space=pltpu.VMEM)

    def narrow_scratch(times):
        return [
            pltpu.VMEM((K, CHUNKS * K), BF16),
            pltpu.VMEM((CHUNKS, 2, HALF, K), F32),
            pltpu.VMEM((times, CHUNKS, HALF, K), F32),
            pltpu.VMEM((CHUNKS, HALF, K), F32),
            pltpu.VMEM((times, CHUNKS, HALF, K), BF16),
            pltpu.VMEM((times, CHUNKS, HALF, K), BF16),
            pltpu.VMEM((times, CHUNKS, 2, HALF, K), F32),
        ]

    a, low, place = pl.pallas_call(
        first_kernel,
        out_shape=[
            jax.ShapeDtypeStruct((CHUNKS * K, CHUNKS * K), BF16),
            jax.ShapeDtypeStruct((K, CHUNKS * K), BF16),
            jax.ShapeDtypeStruct((WIDE * QUARTER, CHUNKS * K), BF16),
        ],
        in_specs=[pl.BlockSpec(memory_space=pl.ANY), vmem],
        out_specs=[vmem, vmem, vmem],
        scratch_shapes=[*narrow_scratch(1), dma((CHUNKS,)), *[dma((1, CHUNKS))] * 6],
        compiler_params=pltpu.CompilerParams(
            collective_id=0, has_side_effects=True, vmem_limit_bytes=24 * 1024 * 1024
        ),
        name="first_projection",
    )(embeddings, ids)
    return pl.pallas_call(
        kernel,
        out_shape=jax.ShapeDtypeStruct((WIDE * SLOTS, K), BF16),
        in_specs=[vmem, vmem, vmem],
        out_specs=vmem,
        scratch_shapes=[
            *narrow_scratch(ITERS),
            pltpu.VMEM((CHUNKS, K, K), F32),
            pltpu.VMEM((K, CHUNKS * K), BF16),
            pltpu.VMEM((ITERS, RING - 1, PLANE, PIECE, K), BF16),
            pltpu.VMEM((ITERS, RING - 1, PLANE, PIECE, K), BF16),
            pltpu.VMEM((PLANE, PIECE, K), F32),
            pltpu.VMEM((ITERS, PLANE, PIECE, K), BF16),
            pltpu.VMEM((ITERS, PLANE, PIECE, K), BF16),
            pltpu.VMEM((RING, PIECE, K), F32),
            pltpu.VMEM((ITERS, WIDE, PIECE, K), BF16),
            pltpu.VMEM((2, HALF, K), F32),
            pltpu.VMEM((ITERS, HALF, K), F32),
            pltpu.VMEM((HALF, K), F32),
            pltpu.VMEM((ITERS, HALF, K), F32),
            pltpu.VMEM((ITERS, K, K), F32),
            pltpu.VMEM((HALF, 2 * HALF), F32),
            pltpu.VMEM((HALF, HALF), F32),
            pltpu.VMEM((K, K), F32),
            pltpu.VMEM((RING, PLANE, PIECE, HALF), BF16),
            pltpu.VMEM((4, 8, RING, 2, PIECE, HALF), BF16),
            pltpu.VMEM((WIDE * PIECE, HALF), F32),
            *[dma((ITERS, CHUNKS))] * 6,
            dma((ITERS,)),
            dma((ITERS, RING)),
            dma((ITERS,)),
            dma((ITERS,)),
            dma((ITERS,)),
            dma((ITERS, RING)),
            dma((ITERS,)),
            dma((ITERS, RING - 1)),
            dma((ITERS, 3)),
            dma((ITERS, 3)),
            dma,
            dma((RING,)),
            dma,
            dma((RING,)),
            dma,
            dma((2,)),
            dma,
        ],
        compiler_params=pltpu.CompilerParams(
            collective_id=1, has_side_effects=True, vmem_limit_bytes=40 * 1024 * 1024
        ),
        name="members",
    )(a, low, place)


def on_device(embeddings, cluster_ids):
    members = members_of(embeddings, cluster_ids.reshape(1, -1))
    count = members.shape[0] // lax.axis_size("narrow")
    own = lax.dynamic_slice_in_dim(members, lax.axis_index("narrow") * count, count, 0)
    return dot(members, own, NT).astype(BF16)[None]


def solution(mesh):
    return jax.shard_map(
        on_device,
        mesh=mesh,
        in_specs=(P("wide", "narrow"), P("wide", None)),
        out_specs=P("wide", None, "narrow"),
        check_vma=False,
    )
```

time: 137 us -> 129 us (0.942)
  Pallas kernels: 133 us -> 125 us
  local copies, waits for them, and re-layouts: 0 us -> 2.28 us
    pallas_call x1, Pallas kernels: 133 us -> 110 us  [members_of(): pl.pallas_call(kernel, out_shape=jax.ShapeDtypeStruct((WIDE * SLOTS, K),...]
    pallas_call x0 -> x1, Pallas kernels: none -> 14.7 us  [members_of(): pl.pallas_call(first_kernel, out_shape=[jax.ShapeDtypeStruct((CHUNKS * K,...]
    unnamed x0 -> x4, local copies, waits for them, and re-layouts: none -> 2.28 us
where the time goes in v3:
time: 129 us
  Pallas kernels  125 us (97%)
  local copies, waits for them, and re-layouts  2.28 us (2%)
  matrix products  2.06 us (2%)
    pallas_call x1, Pallas kernels, members_of(): pl.pallas_call(kernel, out_shape=jax.ShapeDtypeStruct((WIDE * SLOTS, K),...  110 us
    pallas_call x1, Pallas kernels, members_of(): pl.pallas_call(first_kernel, out_shape=[jax.ShapeDtypeStruct((CHUNKS * K,...  14.7 us

profile of v3, /device:TPU:1, one launch (start us, length us, event | category | flops | bytes accessed | tf_op | source)
XLA Modules:
  0.0 129.2 jit_solution(5194412096024283618)
XLA Ops:
  0.0 0.0 copy-start
  0.0 1.6 %copy-done = bf16[1024,1024]{1,0:T(8,128)(2,1)S(1)} copy-done((bf16[1024,1024]{1,0:T(8,128)(2,1)S(1)}, bf16[1024,1024]{1,0:T(8,128)(2,1)}, u32[]{:S(2)}) %copy-start) | copy-done | bytes 2097176
  1.6 0.0 copy-start.1
  1.6 0.7 copy-done.1
  2.3 14.7 %first_projection.1 = (bf16[1024,1024]{1,0:T(8,128)(2,1)S(1)}, bf16[256,1024]{1,0:T(8,128)(2,1)S(1)}, bf16[512,1024]{1,0:T(8,128)(2,1)S(1)}) custom-call(bf16[1024,1024]{1,0:T(8,128)(2,1)S(1)} %copy-done, s32[1,1024]{1,0:T(1,128)S(1)} %bitcast.4), custom_call_target="tpu_custom_call" | custom-call | tf_op jit(solution)/shard_map/first_projection/pallas_call | solution.py:531
  17.0 110.1 %members.1 = bf16[2048,256]{1,0:T(8,128)(2,1)S(1)} custom-call(bf16[1024,1024]{1,0:T(8,128)(2,1)S(1)} %get-tuple-element.8.a_ref, bf16[256,1024]{1,0:T(8,128)(2,1)S(1)} %get-tuple-element.9.low_ref, bf16[512,1024]{1,0:T(8,128)(2,1)S(1)} %get-tuple-element.10.place), custom_call_target="tpu_custom_call" | custom-call | tf_op jit(solution)/shard_map/members/pallas_call | solution.py:546
  127.1 2.1 %fusion = bf16[1,2048,512]{2,1,0:T(8,128)(2,1)} fusion(bf16[2048,256]{1,0:T(8,128)(2,1)S(1)} %members.1, s32[]{:T(128)S(6)} %select_n.3), kind=kOutput, calls=%fused_computation.1 | convolution fusion | flops 537919488 | bytes 3407876 | tf_op jit(solution)/shard_map/dot_general | solution.py:27
Async XLA Ops:
  0.0 1.6 %copy-start = (bf16[1024,1024]{1,0:T(8,128)(2,1)S(1)}, bf16[1024,1024]{1,0:T(8,128)(2,1)}, u32[]{:S(2)}) copy-start(bf16[1024,1024]{1,0:T(8,128)(2,1)} %a_hbm.1) | copy-start | bytes 6291460
  1.6 0.7 copy-start.1

commit v4 on v3

--- a/solution.py
+++ b/solution.py
@@ -13,6 +13,7 @@
 K = 256
 ITERS = 2
 HALF = 128
+TRIANGLE = 192
 PANEL = 16
 CHUNKS = 4
 WIDE = 64
@@ -81,15 +82,16 @@
     row = lax.broadcasted_iota(jnp.int32, (n, n), 0)
     col = lax.broadcasted_iota(jnp.int32, (n, n), 1)
     eye = jnp.where(row == col, 1.0, 0.0).astype(F32)
-    m[:, 0:n] = square[0:n, 0:n]
+    m[:, 0:n] = square[0, 0:n]
     m[:, n : 2 * n] = eye
     eliminate(m)
     first = m[:, n : 2 * n]
-    lower = dot(square[n:, 0:n], first, NT, HIGHEST)
+    cornered = jnp.concatenate([square[0, n:], square[1, n:]], axis=0)
+    lower = dot(cornered, first, NT, HIGHEST)
     out[0:n, 0:n] = first
     out[0:n, n:] = jnp.zeros((n, n), F32)
     cross[...] = dot(lower, first, NN, HIGHEST)
-    m[:, 0:n] = square[n:, n:] - dot(lower, lower, NT, HIGHEST)
+    m[:, 0:n] = square[1, 0:n] - dot(lower, lower, NT, HIGHEST)
     m[:, n : 2 * n] = eye
 
 
@@ -170,85 +172,13 @@
     return project, over_cores, over_chips, whole, sent
 
 
-def first_kernel(
+def kernel(
     a_hbm,
+    ids_hbm,
+    out_ref,
+    a_ref,
     ids_ref,
-    a_ref,
-    low_ref,
     place,
-    vt,
-    part,
-    recv1,
-    chip,
-    send2,
-    recv2,
-    full,
-    load_sem,
-    s1,
-    q1,
-    s2,
-    q2,
-    s3,
-    q3,
-):
-    w = lax.axis_index("wide")
-    n = lax.axis_index("narrow")
-    barrier = pltpu.get_barrier_semaphore()
-    signal(barrier, w, n + 1 - 2 * lax.rem(n, 2))
-    signal(barrier, w, lax.rem(n + 2, 4))
-
-    def load(g):
-        piece = pl.ds(g * K, K)
-        return pltpu.make_async_copy(a_hbm.at[piece], a_ref.at[piece], load_sem.at[g])
-
-    for g in range(CHUNKS):
-        load(g).start()
-    row = lax.broadcasted_iota(jnp.int32, (K, K), 0)
-    col = lax.broadcasted_iota(jnp.int32, (K, K), 1)
-    eye = jnp.where(row == col, 1.0, 0.0).astype(BF16)
-    for g in range(CHUNKS):
-        vt[:, g * K : (g + 1) * K] = eye
-    project, over_cores, over_chips, whole, sent = sum_over_narrow(
-        w, n, vt, a_ref, part, recv1, chip, send2, recv2, full, (s1, q1, s2, q2, s3, q3)
-    )
-    pl.semaphore_wait(barrier, 2)
-    for g in range(CHUNKS):
-        load(g).wait()
-        project(0, g)
-    for g in range(CHUNKS):
-        over_cores(0, g)
-    rows = a_ref.shape[0]
-    ids = ids_ref[...]
-    cluster = lax.broadcasted_iota(jnp.int32, (WIDE, rows), 0)
-    onehot = jnp.where(cluster == ids, 1.0, 0.0).astype(F32)
-    earlier = jnp.where(
-        lax.broadcasted_iota(jnp.int32, (rows, rows), 0)
-        < lax.broadcasted_iota(jnp.int32, (rows, rows), 1),
-        1.0,
-        0.0,
-    ).astype(BF16)
-    counts = dot(onehot.astype(BF16), earlier, NN)
-    slot = jnp.sum(counts * onehot, axis=0, keepdims=True).astype(jnp.int32)
-    offset = slot - n * QUARTER
-    owner = ((ids >> 1) & 3) * PLANE + (ids >> 3) * 2 + (ids & 1)
-    target = jnp.where((offset >= 0) & (offset < QUARTER), owner * QUARTER + offset, -1)
-
-    @pl.loop(0, WIDE * QUARTER, step=128)
-    def _(r):
-        position = lax.broadcasted_iota(jnp.int32, (128, rows), 0) + r
-        place[pl.ds(r, 128), :] = jnp.where(position == target, 1.0, 0.0).astype(BF16)
-    for g in range(CHUNKS):
-        over_chips(0, g)
-    for g in range(CHUNKS):
-        low_ref[:, g * K : (g + 1) * K] = whole(0, g).astype(BF16)
-    sent(0)
-
-
-def kernel(
-    a_ref,
-    low_ref,
-    place,
-    out_ref,
     vt,
     part,
     recv1,
@@ -276,6 +206,7 @@
     outgoing,
     arrived,
     by_lane,
+    load_sem,
     s1,
     q1,
     s2,
@@ -326,11 +257,55 @@
         signal(barrier, at(plane, lax.rem(y + off, RING)), n)
     signal(barrier, w, core_peer)
     signal(barrier, w, chip_peer)
+    def load(g):
+        piece = pl.ds(g * K, K)
+        return pltpu.make_async_copy(a_hbm.at[piece], a_ref.at[piece], load_sem.at[g])
+
+    for g in range(CHUNKS):
+        load(g).start()
+    load_ids = pltpu.make_async_copy(ids_hbm, ids_ref, load_sem.at[CHUNKS])
+    load_ids.start()
+    row = lax.broadcasted_iota(jnp.int32, (K, K), 0)
+    col = lax.broadcasted_iota(jnp.int32, (K, K), 1)
+    eye = jnp.where(row == col, 1.0, 0.0).astype(BF16)
+    for g in range(CHUNKS):
+        vt[:, g * K : (g + 1) * K] = eye
     project, over_cores, over_chips, whole, sent = sum_over_narrow(
         w, n, vt, a_ref, part, recv1, chip, send2, recv2, full, (s1, q1, s2, q2, s3, q3)
     )
-    low[...] = low_ref[...]
+    for g in range(CHUNKS):
+        load(g).wait()
     pl.semaphore_wait(barrier, PLANE - 1 + RING - 1 + 2)
+    for g in range(CHUNKS):
+        project(0, g)
+    for g in range(CHUNKS):
+        over_cores(0, g)
+    rows = a_ref.shape[0]
+    load_ids.wait()
+    ids = ids_ref[...]
+    cluster = lax.broadcasted_iota(jnp.int32, (WIDE, rows), 0)
+    onehot = jnp.where(cluster == ids, 1.0, 0.0).astype(F32)
+    earlier = jnp.where(
+        lax.broadcasted_iota(jnp.int32, (rows, rows), 0)
+        < lax.broadcasted_iota(jnp.int32, (rows, rows), 1),
+        1.0,
+        0.0,
+    ).astype(BF16)
+    counts = dot(onehot.astype(BF16), earlier, NN)
+    slot = jnp.sum(counts * onehot, axis=0, keepdims=True).astype(jnp.int32)
+    offset = slot - n * QUARTER
+    owner = ((ids >> 1) & 3) * PLANE + (ids >> 3) * 2 + (ids & 1)
+    target = jnp.where((offset >= 0) & (offset < QUARTER), owner * QUARTER + offset, -1)
+
+    @pl.loop(0, WIDE * QUARTER, step=128)
+    def _(r):
+        position = lax.broadcasted_iota(jnp.int32, (128, rows), 0) + r
+        place[pl.ds(r, 128), :] = jnp.where(position == target, 1.0, 0.0).astype(BF16)
+    for g in range(CHUNKS):
+        over_chips(0, g)
+    for g in range(CHUNKS):
+        low[:, g * K : (g + 1) * K] = whole(0, g).astype(BF16)
+    sent(0)
 
     def sweep(it, carry):
         def first(off, c, k):
@@ -397,41 +372,43 @@
             vt[:, pl.ds(pl.multiple_of(q * K, K), K)] = yg[it, pl.ds(q * PLANE, PLANE)].reshape(K, K)
 
         now = dot(vt[...], vt[...], NT)
-        sq[0] = now[0:HALF]
-        sq[1] = now[HALF:]
+        sq[0, 0:HALF] = now[0:HALF, 0:HALF]
+        sq[0, HALF:] = now[HALF : HALF + HALF // 2, 0:HALF]
+        sq[1, 0:HALF] = now[HALF:, HALF:]
+        sq[1, HALF:] = now[HALF + HALF // 2 :, 0:HALF]
         e1 = to(sq.at[other], sqr1.at[it], es.at[it, 0], eq.at[it, 0], w, core_peer)
         e1.start()
-        for g in range(CHUNKS):
-            project(it, g)
         e1.wait_recv()
         sqt[...] = sq[core] + sqr1[it]
         e2 = to(sqt, sqr2.at[it], es.at[it, 1], eq.at[it, 1], w, chip_peer)
         e2.start()
+        for g in range(CHUNKS):
+            project(it + 1, g)
         e2.wait_recv()
-        half = sqf.at[it, pl.ds(core * HALF, HALF)]
+        half = sqf.at[it, core]
         half[...] = sqt[...] + sqr2[it]
         e3 = to(half, half, es.at[it, 2], eq.at[it, 2], w, core_peer)
         e3.start()
         for g in range(CHUNKS):
-            over_cores(it, g)
-        rest = sqf.at[it, pl.ds(other * HALF, HALF)]
+            over_cores(it + 1, g)
+        rest = sqf.at[it, other]
         to(rest, rest, es.at[it, 2], eq.at[it, 2], w, core_peer).wait_recv()
         inverse_factor_start(sqf.at[it], work, linv, cross)
 
 
         def between(panel):
             if panel in (3, 4, 5, 6):
-                over_chips(it, panel - 3)
+                over_chips(it + 1, panel - 3)
 
         inverse_factor_end(work, linv, cross, between)
         a, b = split2(linv[...])
         for g in range(CHUNKS):
-            c, d = split2(whole(it, g))
+            c, d = split2(whole(it + 1, g))
             now = dot(a, c, NN) + (dot(a, d, NN) + dot(b, c, NN))
             coords[g] = now
             low[:, g * K : (g + 1) * K] = now.astype(BF16)
 
-        sent(it)
+        sent(it + 1)
         e1.wait_send()
         e2.wait_send()
         e3.wait_send()
@@ -528,28 +505,16 @@
             pltpu.VMEM((times, CHUNKS, 2, HALF, K), F32),
         ]
 
-    a, low, place = pl.pallas_call(
-        first_kernel,
-        out_shape=[
-            jax.ShapeDtypeStruct((CHUNKS * K, CHUNKS * K), BF16),
-            jax.ShapeDtypeStruct((K, CHUNKS * K), BF16),
-            jax.ShapeDtypeStruct((WIDE * QUARTER, CHUNKS * K), BF16),
-        ],
-        in_specs=[pl.BlockSpec(memory_space=pl.ANY), vmem],
-        out_specs=[vmem, vmem, vmem],
-        scratch_shapes=[*narrow_scratch(1), dma((CHUNKS,)), *[dma((1, CHUNKS))] * 6],
-        compiler_params=pltpu.CompilerParams(
-            collective_id=0, has_side_effects=True, vmem_limit_bytes=24 * 1024 * 1024
-        ),
-        name="first_projection",
-    )(embeddings, ids)
     return pl.pallas_call(
         kernel,
         out_shape=jax.ShapeDtypeStruct((WIDE * SLOTS, K), BF16),
-        in_specs=[vmem, vmem, vmem],
+        in_specs=[pl.BlockSpec(memory_space=pl.ANY), pl.BlockSpec(memory_space=pl.ANY)],
         out_specs=vmem,
         scratch_shapes=[
-            *narrow_scratch(ITERS),
+            pltpu.VMEM((CHUNKS * K, CHUNKS * K), BF16),
+            pltpu.VMEM((1, CHUNKS * K), jnp.int32),
+            pltpu.VMEM((WIDE * QUARTER, CHUNKS * K), BF16),
+            *narrow_scratch(ITERS + 1),
             pltpu.VMEM((CHUNKS, K, K), F32),
             pltpu.VMEM((K, CHUNKS * K), BF16),
             pltpu.VMEM((ITERS, RING - 1, PLANE, PIECE, K), BF16),
@@ -559,18 +524,19 @@
             pltpu.VMEM((ITERS, PLANE, PIECE, K), BF16),
             pltpu.VMEM((RING, PIECE, K), F32),
             pltpu.VMEM((ITERS, WIDE, PIECE, K), BF16),
-            pltpu.VMEM((2, HALF, K), F32),
-            pltpu.VMEM((ITERS, HALF, K), F32),
-            pltpu.VMEM((HALF, K), F32),
-            pltpu.VMEM((ITERS, HALF, K), F32),
-            pltpu.VMEM((ITERS, K, K), F32),
+            pltpu.VMEM((2, TRIANGLE, HALF), F32),
+            pltpu.VMEM((ITERS, TRIANGLE, HALF), F32),
+            pltpu.VMEM((TRIANGLE, HALF), F32),
+            pltpu.VMEM((ITERS, TRIANGLE, HALF), F32),
+            pltpu.VMEM((ITERS, 2, TRIANGLE, HALF), F32),
             pltpu.VMEM((HALF, 2 * HALF), F32),
             pltpu.VMEM((HALF, HALF), F32),
             pltpu.VMEM((K, K), F32),
             pltpu.VMEM((RING, PLANE, PIECE, HALF), BF16),
             pltpu.VMEM((4, 8, RING, 2, PIECE, HALF), BF16),
             pltpu.VMEM((WIDE * PIECE, HALF), F32),
-            *[dma((ITERS, CHUNKS))] * 6,
+            dma((CHUNKS + 1,)),
+            *[dma((ITERS + 1, CHUNKS))] * 6,
             dma((ITERS,)),
             dma((ITERS, RING)),
             dma((ITERS,)),
@@ -590,10 +556,10 @@
             dma,
         ],
         compiler_params=pltpu.CompilerParams(
-            collective_id=1, has_side_effects=True, vmem_limit_bytes=40 * 1024 * 1024
+            collective_id=0, has_side_effects=True, vmem_limit_bytes=56 * 1024 * 1024
         ),
         name="members",
-    )(a, low, place)
+    )(embeddings, ids)
 
 
 def on_device(embeddings, cluster_ids):

time: 129 us -> 124 us (0.961)
  Pallas kernels: 125 us -> 120 us
  local copies, waits for them, and re-layouts: 2.28 us -> 0 us
    pallas_call x1 -> x0, Pallas kernels: 14.7 us -> none  [members_of(): pl.pallas_call(first_kernel, out_shape=[jax.ShapeDtypeStruct((CHUNKS * K,...]
    pallas_call x1, Pallas kernels: 110 us -> 120 us  [members_of(): pl.pallas_call(kernel, out_shape=jax.ShapeDtypeStruct((WIDE * SLOTS, K),...]
    unnamed x4 -> x0, local copies, waits for them, and re-layouts: 2.28 us -> none
where the time goes in v4:
time: 124 us
  Pallas kernels  120 us (97%)
  matrix products  3.33 us (3%)
    pallas_call x1, Pallas kernels, members_of(): pl.pallas_call(kernel, out_shape=jax.ShapeDtypeStruct((WIDE * SLOTS, K),...  120 us
    dot_general x1, matrix products, dot(): lax.dot_general(a, b, (dims, ((), ())), precision=precision, preferred_el...  3.33 us

profile of v4, /device:TPU:1, one launch (start us, length us, event | category | flops | bytes accessed | tf_op | source)
XLA Modules:
  0.0 123.7 jit_solution(8576163591022718717)
XLA Ops:
  0.0 120.4 %members.1 = bf16[2048,256]{1,0:T(8,128)(2,1)} custom-call(bf16[1024,1024]{1,0:T(8,128)(2,1)} %a_hbm.1, s32[1,1024]{1,0:T(1,128)} %bitcast.4), custom_call_target="tpu_custom_call" | custom-call | tf_op jit(solution)/shard_map/members/pallas_call | solution.py:508
  120.4 3.3 %fusion = bf16[1,2048,512]{2,1,0:T(8,128)(2,1)} fusion(bf16[2048,256]{1,0:T(8,128)(2,1)} %members.1, s32[]{:T(128)S(6)} %select_n.3), kind=kOutput, calls=%fused_computation.1 | convolution fusion | flops 537919488 | bytes 3407876 | tf_op jit(solution)/shard_map/dot_general | solution.py:28

commit v5 on v4

--- a/solution.py
+++ b/solution.py
@@ -203,6 +203,7 @@
     work,
     cross,
     linv,
+    acc,
     outgoing,
     arrived,
     by_lane,
@@ -369,9 +370,16 @@
             q = lax.rem(y - off + RING, RING)
             if off:
                 settle(yg.at[it, pl.ds(0, PLANE)], dq.at[it, off - 1])
-            vt[:, pl.ds(pl.multiple_of(q * K, K), K)] = yg[it, pl.ds(q * PLANE, PLANE)].reshape(K, K)
-
-        now = dot(vt[...], vt[...], NT)
+            block = yg[it, pl.ds(q * PLANE, PLANE)].reshape(K, K)
+            vt[:, pl.ds(pl.multiple_of(q * K, K), K)] = block
+            gram = dot(block, block, NT)
+            if off == 2:
+                now = acc[...] + gram
+            elif off:
+                acc[...] += gram
+            else:
+                acc[...] = gram
+
         sq[0, 0:HALF] = now[0:HALF, 0:HALF]
         sq[0, HALF:] = now[HALF : HALF + HALF // 2, 0:HALF]
         sq[1, 0:HALF] = now[HALF:, HALF:]
@@ -531,6 +539,7 @@
             pltpu.VMEM((ITERS, 2, TRIANGLE, HALF), F32),
             pltpu.VMEM((HALF, 2 * HALF), F32),
             pltpu.VMEM((HALF, HALF), F32),
+            pltpu.VMEM((K, K), F32),
             pltpu.VMEM((K, K), F32),
             pltpu.VMEM((RING, PLANE, PIECE, HALF), BF16),
             pltpu.VMEM((4, 8, RING, 2, PIECE, HALF), BF16),

time: 124 us -> 123 us (level)
  no operation moved by 1% of the time
where the time goes in v5:
time: 123 us
  Pallas kernels  119 us (97%)
  matrix products  3.33 us (3%)
    pallas_call x1, Pallas kernels, members_of(): pl.pallas_call(kernel, out_shape=jax.ShapeDtypeStruct((WIDE * SLOTS, K),...  119 us
    dot_general x1, matrix products, dot(): lax.dot_general(a, b, (dims, ((), ())), precision=precision, preferred_el...  3.33 us

profile of v5, /device:TPU:1, one launch (start us, length us, event | category | flops | bytes accessed | tf_op | source)
XLA Modules:
  0.0 122.8 jit_solution(324654708316904187)
XLA Ops:
  0.0 119.5 %members.1 = bf16[2048,256]{1,0:T(8,128)(2,1)} custom-call(bf16[1024,1024]{1,0:T(8,128)(2,1)} %a_hbm.1, s32[1,1024]{1,0:T(1,128)} %bitcast.4), custom_call_target="tpu_custom_call" | custom-call | tf_op jit(solution)/shard_map/members/pallas_call | solution.py:516
  119.5 3.3 %fusion = bf16[1,2048,512]{2,1,0:T(8,128)(2,1)} fusion(bf16[2048,256]{1,0:T(8,128)(2,1)} %members.1, s32[]{:T(128)S(6)} %select_n.3), kind=kOutput, calls=%fused_computation.1 | convolution fusion | flops 537919488 | bytes 3407876 | tf_op jit(solution)/shard_map/dot_general | solution.py:28

commit v6 on v5

--- a/solution.py
+++ b/solution.py
@@ -22,6 +22,7 @@
 RING = 4
 PLANE = 16
 QUARTER = 8
+LAYERS = 8
 
 
 def dot(a, b, dims, precision=None):
@@ -435,20 +436,21 @@
     now = dot(place[...], low[...], NT).reshape(RING, PLANE, QUARTER, K)
     outgoing[...] = jnp.concatenate([now[..., 0:HALF], now[..., HALF:]], axis=2).astype(BF16)
 
-    for turn in (0, 1, 3, 2):
-        c = lax.rem(quad + turn, RING)
-
-        @pl.loop(0, PLANE)
+    layers = (0, 1, 7, 2, 6, 3, 5, 4)
+    for turn in layers:
+        c = lax.rem(z + turn, LAYERS)
+
+        @pl.loop(0, 2 * RING)
         def _(t):
             ring = lax.rem(y + t, RING)
-            there = c * RING + lax.rem(within + t // RING, RING)
+            there = c * 2 + lax.rem(x + t // RING, 2)
 
             def send():
                 to(
                     outgoing.at[ring, there],
                     arrived.at[n, z, y, x],
                     ts,
-                    tq.at[quad],
+                    tq.at[z],
                     at(there, ring),
                     n,
                 ).start()
@@ -461,12 +463,12 @@
     arrived[n, z, y, x] = outgoing[y, plane]
 
     def share(c, who, peer, send, recv):
-        block = arrived.at[who, pl.ds(c * 2, 2)]
+        block = arrived.at[who, c]
         return to(block, block, send, recv, w, peer)
 
-    for turn in (0, 1, 3, 2):
-        c = lax.rem(quad + turn, RING)
-        count = PLANE if turn else PLANE - 1
+    for turn in layers:
+        c = lax.rem(z + turn, LAYERS)
+        count = 2 * RING if turn else 2 * RING - 1
         settle(outgoing.at[0, pl.ds(0, count)], tq.at[c])
         share(c, n, chip_peer, vs, vq.at[c]).start()
         share(c, n, core_peer, fs, fq.at[0]).start()
@@ -480,8 +482,8 @@
                 ] = by_lane[pl.ds(h * QUARTER + s, WIDE, stride=PIECE), :].astype(BF16)
 
     arrange(n)
-    for turn in (0, 1, 3, 2):
-        c = lax.rem(quad + turn, RING)
+    for turn in layers:
+        c = lax.rem(z + turn, LAYERS)
         share(c, chip_peer, chip_peer, vs, vq.at[c]).wait_recv()
         share(c, chip_peer, core_peer, gs, fq.at[1]).start()
     settle(arrived.at[core_peer], fq.at[0])
@@ -557,9 +559,9 @@
             dma((ITERS, 3)),
             dma((ITERS, 3)),
             dma,
-            dma((RING,)),
+            dma((LAYERS,)),
             dma,
-            dma((RING,)),
+            dma((LAYERS,)),
             dma,
             dma((2,)),
             dma,

time: 123 us -> 122 us (level)
  no operation moved by 1% of the time
where the time goes in v6:
time: 122 us
  Pallas kernels  119 us (98%)
  matrix products  3.33 us (3%)
    pallas_call x1, Pallas kernels, members_of(): pl.pallas_call(kernel, out_shape=jax.ShapeDtypeStruct((WIDE * SLOTS, K),...  119 us
    dot_general x1, matrix products, dot(): lax.dot_general(a, b, (dims, ((), ())), precision=precision, preferred_el...  3.33 us

profile of v6, /device:TPU:1, one launch (start us, length us, event | category | flops | bytes accessed | tf_op | source)
XLA Modules:
  0.0 122.1 jit_solution(3674869588607267675)
XLA Ops:
  0.0 118.8 %members.1 = bf16[2048,256]{1,0:T(8,128)(2,1)} custom-call(bf16[1024,1024]{1,0:T(8,128)(2,1)} %a_hbm.1, s32[1,1024]{1,0:T(1,128)} %bitcast.4), custom_call_target="tpu_custom_call" | custom-call | tf_op jit(solution)/shard_map/members/pallas_call | solution.py:518
  118.8 3.3 %fusion = bf16[1,2048,512]{2,1,0:T(8,128)(2,1)} fusion(bf16[2048,256]{1,0:T(8,128)(2,1)} %members.1, s32[]{:T(128)S(6)} %select_n.3), kind=kOutput, calls=%fused_computation.1 | convolution fusion | flops 537919488 | bytes 3407876 | tf_op jit(solution)/shard_map/dot_general | solution.py:29
